TPU v7x, 256 devices: a whole 4x4x8 slice. The times are simulated.
256 devices in a mesh: sensor: 32 (over y, x, z_lo), basis: 8 (over z_hi, core).
Axes of the slice: x: 4, y: 4, z: 8 (z_hi: 4, z_lo: 2; z = z_hi * 2 + z_lo), core: 2. Of those that a mesh axis runs over, the one named last changes fastest.
Arguments:
- readings: bfloat16 [98304, 128], P('sensor'), may hold values from -120 to 120
- design_tiles: bfloat16 [96, 8, 2, 1024, 512], P('sensor', 'basis'), may hold values from -0.0625 to 0.0625
- pattern: int32 [96, 8, 2], P('sensor', 'basis'), may hold values from 0 to 7, as said below
Outputs:
- solution: float32 [32768, 128], P('basis')
- search: float32 [32768, 128], P('basis')
- phi_bar: float32 [128], replicated
Inputs may be any that keep to these rules, and one draw needn't show every extreme that they name: `pattern`: within one segment and one basis group the 2 entries are different.
All inputs are finite; a program needn't handle non-finite values.
Results may differ from a plain program's by a relative error of at most 0.02.
Values may be sent and summed in bfloat16 or wider, within the bound.
No kernel may reach another device: no remote copies, remote signals or barrier semaphores. Data moves between devices by JAX's collectives and lax.ppermute only.
A program may use at most 64 MiB of HBM per device.

v0:
```python
import jax
import jax.numpy as jnp
from jax import lax
from jax.sharding import PartitionSpec as P

CB_DEV = 8
ITERS = 3


epsilon = 1e-06


def per_device(readings, design_tiles, pattern):
    rows_loc = readings.shape[0]
    rhs_cols = readings.shape[1]
    blocks_dev = design_tiles.shape[0]
    slots = design_tiles.shape[2]
    seg_rows = design_tiles.shape[3]
    block_cols = design_tiles.shape[4]
    tile_set = design_tiles.reshape(blocks_dev, slots, seg_rows, block_cols)
    slot_ids = pattern.reshape(blocks_dev * slots)
    selector = (jnp.arange(CB_DEV, dtype=jnp.int32)[:, None] == slot_ids[None, :]).astype(
        jnp.float32
    )

    def times_transpose(left_bf):
        contrib = jnp.einsum(
            "rjsb,rsk->rjbk",
            tile_set,
            left_bf.reshape(blocks_dev, seg_rows, rhs_cols),
            preferred_element_type=jnp.float32,
        )
        summed = jnp.dot(
            selector,
            contrib.reshape(blocks_dev * slots, block_cols * rhs_cols),
            precision=lax.Precision.HIGHEST,
        )
        return summed.reshape(CB_DEV * block_cols, rhs_cols)

    def row_norm(left_vec):
        local = jnp.sum(left_vec * left_vec, axis=0)
        total = lax.psum(local, "sensor")
        return jnp.sqrt(total + epsilon)

    def row_operand(left_vec):
        narrow = left_vec.astype(jnp.bfloat16)
        return narrow

    def column_total(left_bf):
        shares = lax.psum_scatter(
            times_transpose(left_bf), "sensor", scatter_dimension=0, tiled=True
        )
        return lax.all_gather(shares, "sensor", axis=0, tiled=True)

    def column_norm(right_vec):
        local = jnp.sum(right_vec * right_vec, axis=0)
        total = lax.psum(local, "basis")
        return jnp.sqrt(total + epsilon)

    start = readings.astype(jnp.float32)
    beta_col = row_norm(start)
    left_vec = start / beta_col
    right_vec = column_total(row_operand(left_vec))
    alpha_col = column_norm(right_vec)
    right_vec = right_vec / alpha_col
    search = right_vec
    solution = jnp.zeros_like(right_vec)
    phi_bar = beta_col
    rho_bar = alpha_col
    for sweep in range(ITERS):
        column_narrow = right_vec.astype(jnp.bfloat16)
        picked = jnp.take(column_narrow.reshape(CB_DEV, block_cols, rhs_cols), slot_ids, axis=0)
        picked = picked.reshape(blocks_dev, slots, block_cols, rhs_cols)
        images = jnp.einsum("rjsb,rjbk->rsk", tile_set, picked, preferred_element_type=jnp.float32)
        partial_rows = images.reshape(rows_loc, rhs_cols)
        left_vec = lax.psum(partial_rows, "basis") - alpha_col * left_vec
        beta_col = row_norm(left_vec)
        left_vec = left_vec / beta_col
        right_vec = column_total(row_operand(left_vec)) - beta_col * right_vec
        alpha_col = column_norm(right_vec)
        right_vec = right_vec / alpha_col
        rho_col = jnp.sqrt(rho_bar * rho_bar + beta_col * beta_col)
        cosine = rho_bar / rho_col
        sine = beta_col / rho_col
        theta_col = sine * alpha_col
        rho_bar = -cosine * alpha_col
        phi_col = cosine * phi_bar
        phi_bar = sine * phi_bar
        solution = solution + phi_col / rho_col * search
        search = right_vec - theta_col / rho_col * search
    return (solution, search, phi_bar)


def solution(mesh):
    placed = (P("sensor", None), P("sensor", "basis", None, None, None), P("sensor", "basis", None))
    return jax.shard_map(
        per_device,
        mesh=mesh,
        in_specs=placed,
        out_specs=(P("basis", None), P("basis", None), P()),
        check_vma=False,
    )
```

profile of v0, /device:TPU:1, one launch (start us, length us, event | category | flops | bytes accessed | tf_op | source)
XLA Modules:
  0.0 2053.6 jit_solution(10937164230212609368)
XLA Ops:
  7.2 1.6 fusion.26
  8.8 70.5 %psum.77 = f32[128]{0:T(128)S(1)} all-reduce(f32[128]{0:T(128)S(1)} %fusion.26), channel_id=1, replica_groups=mesh['sensor'=32,'basis'=8] {'sensor'}, use_global_device_ids=true, to_apply=%region_1.0 | all-reduce | flops 128 | bytes 1024 | tf_op jit(solution)/shard_map/psum | solution.py:42
  79.3 0.8 copy.14
  80.2 1.3 fusion.48
  81.5 5.0 fusion.27
  86.5 1.9 copy.16
  88.3 3.2 fusion.23
  91.5 3.2 reshape.96
  94.8 156.1 %reduce-scatter.5.cloned.1.call-done = f32[128,128]{1,0:T(8,128)} async-done(((f32[4096,128]{1,0:T(8,128)}), f32[128,128]{1,0:T(8,128)}) %reduce-scatter.5.cloned.1.call-update) | async-done | bytes 65552 | tf_op jit(solution)/shard_map/reduce_scatter | solution.py:50
  251.0 158.0 %all-gather.5.cloned.1.call-done = f32[4096,128]{1,0:T(8,128)} async-done(((f32[128,128]{1,0:T(8,128)}), f32[4096,128]{1,0:T(8,128)}) %all-gather.5.cloned.1.call-update) | async-done | bytes 2097168 | tf_op jit(solution)/shard_map/all_gather | solution.py:53
  409.0 2.3 multiply_reduce_fusion.3
  411.3 34.4 %psum.78 = f32[128]{0:T(128)S(1)} all-reduce(f32[128]{0:T(128)S(1)} %multiply_reduce_fusion.3), channel_id=1, replica_groups=mesh['sensor'=32,'basis'=8] {'basis'}, use_global_device_ids=true, to_apply=%region_4.0 | all-reduce | flops 128 | bytes 1024 | tf_op jit(solution)/shard_map/psum | solution.py:57
  445.8 1.6 gather_fusion
  447.4 1.3 broadcast_select_fusion.2
  448.6 6.1 fusion.30
  454.8 3.1 copy.18
  457.9 79.7 %all-reduce.4.cloned.1.call-done = f32[3072,128]{1,0:T(8,128)} async-done(((f32[3072,128]{1,0:T(8,128)}), f32[3072,128]{1,0:T(8,128)}) %all-reduce.4.cloned.1.call-update) | async-done | bytes 1572880 | tf_op jit(solution)/shard_map/psum | solution.py:76
  537.7 1.8 multiply_reduce_fusion.6
  539.5 68.6 %psum.80 = f32[128]{0:T(128)S(1)} all-reduce(f32[128]{0:T(128)S(1)} %multiply_reduce_fusion.6), channel_id=1, replica_groups=mesh['sensor'=32,'basis'=8] {'sensor'}, use_global_device_ids=true, to_apply=%region_7.9 | all-reduce | flops 128 | bytes 1024 | tf_op jit(solution)/shard_map/psum | solution.py:42
  608.1 1.7 fusion.49
  609.8 5.0 fusion.33
  614.8 3.0 copy.20
  617.8 4.6 fusion.20
  622.4 3.2 reshape.102
  625.7 152.4 %reduce-scatter.7.cloned.1.call-done = f32[128,128]{1,0:T(8,128)} async-done(((f32[4096,128]{1,0:T(8,128)}), f32[128,128]{1,0:T(8,128)}) %reduce-scatter.7.cloned.1.call-update) | async-done | bytes 65552 | tf_op jit(solution)/shard_map/reduce_scatter | solution.py:50
  778.3 158.2 %all-gather.7.cloned.1.call-done = f32[4096,128]{1,0:T(8,128)} async-done(((f32[128,128]{1,0:T(8,128)}), f32[4096,128]{1,0:T(8,128)}) %all-gather.7.cloned.1.call-update) | async-done | bytes 2097168 | tf_op jit(solution)/shard_map/all_gather | solution.py:53
  936.5 2.2 multiply_reduce_fusion.2
  938.7 34.4 %psum.81 = f32[128]{0:T(128)S(1)} all-reduce(f32[128]{0:T(128)S(1)} %multiply_reduce_fusion.2), channel_id=1, replica_groups=mesh['sensor'=32,'basis'=8] {'basis'}, use_global_device_ids=true, to_apply=%region_10.12 | all-reduce | flops 128 | bytes 1024 | tf_op jit(solution)/shard_map/psum | solution.py:57
  973.0 3.7 fusion.67
  976.7 2.8 gather_fusion.1
  979.5 1.3 broadcast_select_fusion.1
  980.7 6.1 fusion.36
  986.9 3.0 copy.22
  990.0 79.5 %all-reduce.6.cloned.1.call-done = f32[3072,128]{1,0:T(8,128)} async-done(((f32[3072,128]{1,0:T(8,128)}), f32[3072,128]{1,0:T(8,128)}) %all-reduce.6.cloned.1.call-update) | async-done | bytes 1572880 | tf_op jit(solution)/shard_map/psum | solution.py:76
  1069.5 3.5 multiply_reduce_fusion.5
  1072.9 68.5 %psum.83 = f32[128]{0:T(128)S(1)} all-reduce(f32[128]{0:T(128)S(1)} %get-tuple-element.13), channel_id=1, replica_groups=mesh['sensor'=32,'basis'=8] {'sensor'}, use_global_device_ids=true, to_apply=%region_13.15 | all-reduce | flops 128 | bytes 1024 | tf_op jit(solution)/shard_map/psum | solution.py:42
  1141.5 1.5 fusion.50
  1143.0 5.0 fusion.39
  1148.0 3.0 copy.24
  1151.1 4.6 fusion.17
  1155.7 3.3 reshape.108
  1159.0 152.9 %reduce-scatter.9.cloned.1.call-done = f32[128,128]{1,0:T(8,128)} async-done(((f32[4096,128]{1,0:T(8,128)}), f32[128,128]{1,0:T(8,128)}) %reduce-scatter.9.cloned.1.call-update) | async-done | bytes 65552 | tf_op jit(solution)/shard_map/reduce_scatter | solution.py:50
  1312.0 158.4 %all-gather.9.cloned.1.call-done = f32[4096,128]{1,0:T(8,128)} async-done(((f32[128,128]{1,0:T(8,128)}), f32[4096,128]{1,0:T(8,128)}) %all-gather.9.cloned.1.call-update) | async-done | bytes 2097168 | tf_op jit(solution)/shard_map/all_gather | solution.py:53
  1470.4 2.8 multiply_reduce_fusion.1
  1473.2 34.4 %psum.84 = f32[128]{0:T(128)S(1)} all-reduce(f32[128]{0:T(128)S(1)} %multiply_reduce_fusion.1), channel_id=1, replica_groups=mesh['sensor'=32,'basis'=8] {'basis'}, use_global_device_ids=true, to_apply=%region_16.18 | all-reduce | flops 128 | bytes 1024 | tf_op jit(solution)/shard_map/psum | solution.py:57
  1507.6 2.5 fusion.61
  1510.1 1.6 gather_fusion.2
  1511.7 1.3 broadcast_select_fusion
  1512.9 6.1 fusion.42
  1519.1 3.1 copy.26
  1522.2 79.7 %all-reduce.8.cloned.1.call-done = f32[3072,128]{1,0:T(8,128)} async-done(((f32[3072,128]{1,0:T(8,128)}), f32[3072,128]{1,0:T(8,128)}) %all-reduce.8.cloned.1.call-update) | async-done | bytes 1572880 | tf_op jit(solution)/shard_map/psum | solution.py:76
  1602.0 2.3 multiply_reduce_fusion.4
  1604.3 68.8 %psum.86 = f32[128]{0:T(128)S(1)} all-reduce(f32[128]{0:T(128)S(1)} %multiply_reduce_fusion.4), channel_id=1, replica_groups=mesh['sensor'=32,'basis'=8] {'sensor'}, use_global_device_ids=true, to_apply=%region_19.21 | all-reduce | flops 128 | bytes 1024 | tf_op jit(solution)/shard_map/psum | solution.py:42
  1673.1 0.6 multiply_multiply_fusion
  1673.6 2.2 divide_convert_fusion
  1675.8 5.0 fusion.45
  1680.8 3.0 copy.28
  1683.8 4.6 fusion.14
  1688.5 3.2 reshape.114
  1691.7 153.0 %reduce-scatter.11.cloned.1.call-done = f32[128,128]{1,0:T(8,128)} async-done(((f32[4096,128]{1,0:T(8,128)}), f32[128,128]{1,0:T(8,128)}) %reduce-scatter.11.cloned.1.call-update) | async-done | bytes 65552 | tf_op jit(solution)/shard_map/reduce_scatter | solution.py:50
  1844.8 158.3 %all-gather.11.cloned.1.call-done = f32[4096,128]{1,0:T(8,128)} async-done(((f32[128,128]{1,0:T(8,128)}), f32[4096,128]{1,0:T(8,128)}) %all-gather.11.cloned.1.call-update) | async-done | bytes 2097168 | tf_op jit(solution)/shard_map/all_gather | solution.py:53
  2003.1 3.4 multiply_reduce_fusion
  2006.5 34.4 %psum.87 = f32[128]{0:T(128)S(1)} all-reduce(f32[128]{0:T(128)S(1)} %multiply_reduce_fusion), channel_id=1, replica_groups=mesh['sensor'=32,'basis'=8] {'basis'}, use_global_device_ids=true, to_apply=%region_22.24 | all-reduce | flops 128 | bytes 1024 | tf_op jit(solution)/shard_map/psum | solution.py:57
  2040.9 6.2 multiply_subtract_fusion
  (38 shorter events, 1.2 us)
Async XLA Ops:
  7.2 243.7 %reduce-scatter.5.cloned.1.call-start = ((), (), s32[]{:S(2)}) async-start(), calls=%async_computation.4 | async-start | bytes 2162688 | tf_op jit(solution)/shard_map/reduce_scatter | solution.py:50
  94.7 314.2 %all-gather.5.cloned.1.call-start = ((), (), s32[]{:S(2)}) async-start(), calls=%async_computation.5 | async-start | bytes 2162688 | tf_op jit(solution)/shard_map/all_gather | solution.py:53
  250.9 286.8 %all-reduce.4.cloned.1.call-start = ((), (), s32[]{:S(2)}) async-start(), calls=%async_computation.6 | async-start | bytes 3145728 | tf_op jit(solution)/shard_map/psum | solution.py:76
  409.0 36.7 %copy-start = (f32[4096,128]{1,0:T(8,128)S(1)}, f32[4096,128]{1,0:T(8,128)}, u32[]{:S(2)}) copy-start(f32[4096,128]{1,0:T(8,128)} %all-gather.5.cloned.1.call-done) | copy-start | bytes 6291460
  454.8 82.9 %copy-start.1 = (bf16[3072,128]{1,0:T(8,128)(2,1)S(1)}, bf16[3072,128]{1,0:T(8,128)(2,1)}, u32[]{:S(2)}) copy-start(bf16[3072,128]{1,0:T(8,128)(2,1)} %param.5) | copy-start | bytes 2359300
  457.9 320.2 %reduce-scatter.7.cloned.1.call-start = ((), (), s32[]{:S(2)}) async-start(), calls=%async_computation.7 | async-start | bytes 2162688 | tf_op jit(solution)/shard_map/reduce_scatter | solution.py:50
  625.7 310.8 %all-gather.7.cloned.1.call-start = ((), (), s32[]{:S(2)}) async-start(), calls=%async_computation.8 | async-start | bytes 2162688 | tf_op jit(solution)/shard_map/all_gather | solution.py:53
  778.1 291.3 %all-reduce.6.cloned.1.call-start = ((), (), s32[]{:S(2)}) async-start(), calls=%async_computation.9 | async-start | bytes 3145728 | tf_op jit(solution)/shard_map/psum | solution.py:76
  989.9 322.0 %reduce-scatter.9.cloned.1.call-start = ((), (), s32[]{:S(2)}) async-start(), calls=%async_computation.10 | async-start | bytes 2162688 | tf_op jit(solution)/shard_map/reduce_scatter | solution.py:50
  1159.0 311.5 %all-gather.9.cloned.1.call-start = ((), (), s32[]{:S(2)}) async-start(), calls=%async_computation.11 | async-start | bytes 2162688 | tf_op jit(solution)/shard_map/all_gather | solution.py:53
  1312.0 290.0 %all-reduce.8.cloned.1.call-start = ((), (), s32[]{:S(2)}) async-start(), calls=%async_computation.12 | async-start | bytes 3145728 | tf_op jit(solution)/shard_map/psum | solution.py:76
  1522.2 322.6 %reduce-scatter.11.cloned.1.call-start = ((), (), s32[]{:S(2)}) async-start(), calls=%async_computation.13 | async-start | bytes 2162688 | tf_op jit(solution)/shard_map/reduce_scatter | solution.py:50
  1691.7 311.4 %all-gather.11.cloned.1.call-start = ((), (), s32[]{:S(2)}) async-start(), calls=%async_computation.14 | async-start | bytes 2162688 | tf_op jit(solution)/shard_map/all_gather | solution.py:53
Sparse Core Ops, SparseCore 0:
  94.9 155.9 reduce-scatter.4
  252.8 156.1 all-gather.4
  458.0 79.6 all-reduce.3
  625.8 152.2 reduce-scatter.6
  779.7 156.7 all-gather.6
  990.0 79.3 all-reduce.5
  1159.1 152.8 reduce-scatter.8
  1313.9 156.5 all-gather.8
  1522.3 79.6 all-reduce.7
  1691.8 152.9 reduce-scatter.10
  1846.6 156.4 all-gather.10
where the time goes:
time: 2050 us
  waiting for transfers between devices  1490 us (73%)
  blocking collectives  414 us (20%)
  matrix products  55.4 us (3%)
  other arithmetic  43.6 us (2%)
  local copies, waits for them, and re-layouts  39.8 us (2%)
    all_gather x4, waiting for transfers between devices, column_total(): return lax.all_gather(shares, 'sensor', axis=0, tiled=True)  633 us
    reduce_scatter x4, waiting for transfers between devices, column_total(): lax.psum_scatter(times_transpose(left_bf), 'sensor', scatter_dimension=0,...  614 us
    psum x4, blocking collectives, row_norm(): total = lax.psum(local, 'sensor')  276 us
    psum x3, waiting for transfers between devices, per_device(): left_vec = lax.psum(partial_rows, 'basis') - alpha_col * left_vec  239 us
    psum x4, blocking collectives, column_norm(): total = lax.psum(local, 'basis')  137 us
  transfers between devices with their start and end apart: 11, of which 11 were waited for; matrix products, arithmetic and copies ran while one was open for 0% of the time, Pallas kernels for 0%

commit v1 on v0

v1 whole, which is shorter than its diff:
```python
import functools

import jax
import jax.numpy as jnp
from jax import lax
from jax.experimental import pallas as pl
from jax.experimental.pallas import tpu as pltpu
from jax.sharding import PartitionSpec as P

CB_DEV = 8
ITERS = 3
EPS = 1e-06
LANES = 128
EXTRA = 16
VMEM_LIMIT = 24 * 1024 * 1024

BF = jnp.bfloat16
F32 = jnp.float32
Z_GROUPS = [[0, 2, 4, 6], [1, 3, 5, 7]]
CORE_PERM = [(i, i ^ 1) for i in range(8)]

VM = pl.BlockSpec(memory_space=pltpu.VMEM)
SM = pl.BlockSpec(memory_space=pltpu.SMEM)
ANY = pl.BlockSpec(memory_space=pl.ANY)


def sds(shape, dtype):
    return jax.ShapeDtypeStruct(shape, dtype)


def call(body, ins, outs, scratch=()):
    return pl.pallas_call(
        body,
        in_specs=ins,
        out_specs=[VM] * len(outs),
        out_shape=outs,
        scratch_shapes=scratch,
        compiler_params=pltpu.CompilerParams(vmem_limit_bytes=VMEM_LIMIT),
    )


def pack_row(row):
    high = row.astype(BF).astype(F32)
    low = row - high
    which = lax.broadcasted_iota(jnp.int32, (EXTRA, LANES), 0)
    tile = jnp.where(which == 0, high, jnp.where(which == 1, low, 0.0))
    return tile.astype(BF)


def unpack_rows(tile):
    wide = tile.astype(F32)
    if wide.ndim == 3:
        wide = jnp.sum(wide, axis=0)
    return jnp.sum(wide, axis=0, keepdims=True)


def across(row):
    return jnp.transpose(jnp.broadcast_to(row, (LANES, LANES)))


def tile_copies(tiles_ref, buf, sems, first):
    copies = []
    segs = []
    for i in range(6):
        q = lax.rem(first + i, 6)
        seg = lax.div(q, 2)
        top = pl.multiple_of(lax.rem(q, 2) * 512, 512)
        copies.append(
            pltpu.make_async_copy(tiles_ref.at[seg, :, pl.ds(top, 512), :], buf.at[i], sems.at[i])
        )
        segs.append(seg)
    return copies, segs


def forward_body(core_ref, slot_ref, g_ref, tiles_ref, send_ref, keep_ref, asq_ref, buf, sems):
    core = core_ref[0]
    copies, segs = tile_copies(tiles_ref, buf, sems, 3 * (1 - core))
    for c in copies:
        c.start()
    total = jnp.zeros((LANES, LANES), F32)
    for q in range(32):
        piece = g_ref[q].astype(F32)
        total = total + piece * piece
    asq = jnp.sum(jnp.transpose(total), axis=0, keepdims=True)
    asq_ref[...] = asq
    send_ref[1536:1552, :] = pack_row(asq)
    for i in range(6):
        copies[i].wait()
        acc = None
        for j in range(2):
            base = slot_ref[2 * segs[i] + j] * 4
            operand = jnp.concatenate([g_ref[base + t] for t in range(4)], axis=1)
            part = lax.dot_general(
                buf[i, j], operand, (((1,), (1,)), ((), ())), preferred_element_type=F32
            )
            acc = part if acc is None else acc + part
        if i < 3:
            send_ref[i * 512 : (i + 1) * 512, :] = acc.astype(BF)
        else:
            keep_ref[(i - 3) * 512 : (i - 2) * 512, :] = acc


def merge_body(keep_ref, recv_ref, asq_ref, msg_ref):
    tail = pack_row(asq_ref[...] + unpack_rows(recv_ref[1536:1552, :]))
    for z in range(4):
        part = keep_ref[z * 384 : (z + 1) * 384, :] + recv_ref[z * 384 : (z + 1) * 384, :].astype(F32)
        msg_ref[z, 0:384, :] = part.astype(BF)
        msg_ref[z, 384:400, :] = tail


def left_body(recv_ref, left_ref, bsq_ref, new_ref, msg_ref, asq_ref):
    asq = unpack_rows(recv_ref[:, 384:400, :])
    alpha = jnp.sqrt(asq + EPS)
    beta = jnp.sqrt(bsq_ref[...] + EPS)
    total = recv_ref[0, 0:384, :].astype(F32)
    for z in range(1, 4):
        total = total + recv_ref[z, 0:384, :].astype(F32)
    fresh = total * (1.0 / alpha) - (alpha / beta) * left_ref[...].astype(F32)
    new_ref[...] = fresh
    narrow = fresh.astype(BF)
    for z in range(4):
        msg_ref[z] = narrow
    asq_ref[...] = asq


def backward_body(core_ref, slot_ref, own_ref, other_ref, tiles_ref, msg_ref, buf, acc, sems):
    core = core_ref[0]
    copies, segs = tile_copies(tiles_ref, buf, sems, 3 * core)
    for c in copies:
        c.start()
    acc[...] = jnp.zeros_like(acc)
    bsq = jnp.zeros((1, LANES), F32)
    for ref in (own_ref, other_ref):
        for i in range(3):
            wide = ref[i * 512 : (i + 1) * 512, :].astype(F32)
            bsq = bsq + jnp.sum(wide * wide, axis=0, keepdims=True)
    for i in range(6):
        ref = own_ref if i < 3 else other_ref
        rows = (i % 3) * 512
        chunk = ref[rows : rows + 512, :]
        copies[i].wait()
        for j in range(2):
            slot = slot_ref[2 * segs[i] + j]
            part = lax.dot_general(
                chunk, buf[i, j], (((0,), (0,)), ((), ())), preferred_element_type=F32
            )
            acc[slot] += part
    tail = pack_row(bsq)
    for q in range(32):
        lane = (q % 4) * LANES
        msg_ref[q, 0:128, :] = acc[q // 4, :, lane : lane + LANES].astype(BF)
        msg_ref[q, 128:144, :] = tail


def share_body(first, recv_ref, *refs):
    if first:
        r_ref, msg_ref, bsq_ref = refs
    else:
        prev_ref, asq_ref, r_ref, msg_ref, bsq_ref = refs
    bsq = unpack_rows(recv_ref[:, 128:144, :])
    beta = jnp.sqrt(bsq + EPS)
    total = recv_ref[0, 0:128, :].astype(F32)
    for q in range(1, 32):
        total = total + recv_ref[q, 0:128, :].astype(F32)
    fresh = total * across(1.0 / beta)
    if not first:
        alpha = jnp.sqrt(asq_ref[...] + EPS)
        fresh = fresh - across(beta / alpha) * prev_ref[...]
    r_ref[...] = fresh
    narrow = fresh.astype(BF)
    for q in range(32):
        msg_ref[q] = narrow
    bsq_ref[...] = bsq


def square_body(g_ref, asq_ref):
    total = jnp.zeros((LANES, LANES), F32)
    for q in range(32):
        piece = g_ref[q].astype(F32)
        total = total + piece * piece
    asq_ref[...] = jnp.sum(jnp.transpose(total), axis=0, keepdims=True)


def final_body(coef_ref, g0_ref, g1_ref, g2_ref, g3_ref, sol_ref, search_ref):
    rows = coef_ref[...]
    wide = [across(rows[i : i + 1, :]) for i in range(7)]
    for q in range(32):
        g0 = g0_ref[q].astype(F32)
        g1 = g1_ref[q].astype(F32)
        g2 = g2_ref[q].astype(F32)
        g3 = g3_ref[q].astype(F32)
        sol = wide[0] * g0 + wide[1] * g1 + wide[2] * g2
        search = wide[3] * g0 + wide[4] * g1 + wide[5] * g2 + wide[6] * g3
        sol_ref[q * 128 : (q + 1) * 128, :] = jnp.transpose(sol)
        search_ref[q * 128 : (q + 1) * 128, :] = jnp.transpose(search)


def per_device(readings, design_tiles, pattern):
    tiles = design_tiles.reshape(3, 2, 1024, 512)
    slots = pattern.reshape(6)
    basis = lax.axis_index("basis")
    core = lax.rem(basis, 2).reshape(1).astype(jnp.int32)
    zero = jnp.zeros((1,), jnp.int32)
    z_hi = lax.div(basis, 2)
    sems = pltpu.SemaphoreType.DMA((6,))
    chunk_buf = pltpu.VMEM((6, 2, 512, 512), BF)

    forward = call(
        forward_body,
        [SM, SM, VM, ANY],
        [sds((1552, LANES), BF), sds((1536, LANES), F32), sds((1, LANES), F32)],
        [chunk_buf, sems],
    )
    merge = call(merge_body, [VM] * 3, [sds((4, 400, LANES), BF)])
    left = call(
        left_body,
        [VM] * 3,
        [sds((384, LANES), F32), sds((4, 384, LANES), BF), sds((1, LANES), F32)],
    )
    backward = call(
        backward_body,
        [SM, SM, VM, VM, ANY],
        [sds((32, 144, LANES), BF)],
        [chunk_buf, pltpu.VMEM((8, LANES, 512), F32), sems],
    )
    share_outs = [sds((LANES, LANES), F32), sds((32, LANES, LANES), BF), sds((1, LANES), F32)]
    share_first = call(functools.partial(share_body, True), [VM], share_outs)
    share = call(functools.partial(share_body, False), [VM] * 3, share_outs)

    def over_sensor(msg):
        return lax.all_to_all(msg, "sensor", 0, 0, tiled=True)

    def over_z(msg):
        return lax.all_to_all(msg, "basis", 0, 0, tiled=True, axis_index_groups=Z_GROUPS)

    (msg,) = backward(zero, slots, readings[:1536], readings[1536:], tiles)
    r, msg, bsq = share_first(over_sensor(msg))
    gathered = [over_sensor(msg)]
    bsqs = [bsq]
    asqs = []
    left_rows = lax.dynamic_slice_in_dim(readings, core[0] * 1536 + z_hi * 384, 384, 0)
    left_rows = left_rows.astype(F32)
    for sweep in range(ITERS):
        send, keep, asq = forward(core, slots, gathered[-1], tiles)
        other = lax.ppermute(send, "basis", CORE_PERM)
        (msg,) = merge(keep, other, asq)
        left_rows, msg, asq = left(over_z(msg), left_rows, bsqs[-1])
        asqs.append(asq)
        own = over_z(msg).reshape(1536, LANES)
        other = lax.ppermute(own, "basis", CORE_PERM)
        (msg,) = backward(core, slots, own, other, tiles)
        r, msg, bsq = share(over_sensor(msg), r, asq)
        bsqs.append(bsq)
        gathered.append(over_sensor(msg))
    (asq,) = call(square_body, [VM], [sds((1, LANES), F32)])(gathered[-1])
    asqs.append(lax.psum(asq, "basis"))

    betas = [jnp.sqrt(b + EPS) for b in bsqs]
    alphas = [jnp.sqrt(a + EPS) for a in asqs]
    phi_bar = betas[0]
    rho_bar = alphas[0]
    steps = []
    shifts = []
    for k in range(ITERS):
        beta, alpha = betas[k + 1], alphas[k + 1]
        rho = jnp.sqrt(rho_bar * rho_bar + beta * beta)
        cosine = rho_bar / rho
        sine = beta / rho
        theta = sine * alpha
        rho_bar = -cosine * alpha
        phi = cosine * phi_bar
        phi_bar = sine * phi_bar
        steps.append(phi / rho)
        shifts.append(theta / rho)
    s1, s2, s3 = steps
    t1, t2, t3 = shifts
    coef = jnp.concatenate(
        [
            (s1 - s2 * t1 + s3 * t2 * t1) / alphas[0],
            (s2 - s3 * t2) / alphas[1],
            s3 / alphas[2],
            -(t3 * t2 * t1) / alphas[0],
            t3 * t2 / alphas[1],
            -t3 / alphas[2],
            1.0 / alphas[3],
            jnp.zeros_like(s1),
        ],
        axis=0,
    )
    sol, search = call(
        final_body, [VM] * 5, [sds((4096, LANES), F32), sds((4096, LANES), F32)]
    )(coef, *gathered)
    return sol, search, phi_bar.reshape(LANES)


def solution(mesh):
    placed = (P("sensor", None), P("sensor", "basis", None, None, None), P("sensor", "basis", None))
    return jax.shard_map(
        per_device,
        mesh=mesh,
        in_specs=placed,
        out_specs=(P("basis", None), P("basis", None), P()),
        check_vma=False,
    )
```

time: 2050 us -> 365 us (0.18)
  waiting for transfers between devices: 1490 us -> 50.7 us
  blocking collectives: 414 us -> 228 us
  matrix products: 55.4 us -> 0 us
  other arithmetic: 43.6 us -> 1.56 us
  Pallas kernels: 0 us -> 38.5 us
  starting transfers between devices: 0.63 us -> 28.6 us
  local copies, waits for them, and re-layouts: 39.8 us -> 15.4 us
    all_gather x4 -> x0, waiting for transfers between devices: 633 us -> none  [column_total(): return lax.all_gather(shares, 'sensor', axis=0, tiled=True)]
    reduce_scatter x4 -> x0, waiting for transfers between devices: 614 us -> none  [column_total(): lax.psum_scatter(times_transpose(left_bf), 'sensor', scatter_dimension=0,...]
    psum x8 -> x1, blocking collectives: 414 us -> 16.5 us  [per_device(): asqs.append(lax.psum(asq, 'basis'))]
    psum x3 -> x0, waiting for transfers between devices: 239 us -> none  [per_device(): left_vec = lax.psum(partial_rows, 'basis') - alpha_col * left_vec]
    all_to_all x0 -> x11, blocking collectives: none -> 212 us  [the longest x6 134 us: over_sensor(): return lax.all_to_all(msg, 'sensor', 0, 0, tiled=True)]
    dot_general x11 -> x0, matrix products: 55.4 us -> none  [the longest x4 20 us: times_transpose(): jnp.einsum('rjsb,rsk->rjbk', tile_set, left_bf.reshape(blocks_dev, seg_ro...]
    all_to_all x0 -> x3, waiting for transfers between devices: none -> 42.6 us  [the longest x2 31.2 us: over_sensor(): return lax.all_to_all(msg, 'sensor', 0, 0, tiled=True)]
    pallas_call x0 -> x19, Pallas kernels: none -> 38.5 us  [the longest x3 16.4 us: per_device(): send, keep, asq = forward(core, slots, gathered[-1], tiles)]
  transfers between devices with their start and end apart: 11 -> 9, of which waited for: 11 -> 9; matrix products, arithmetic and copies ran while one was open for 0% -> 0% of each run, Pallas kernels for 0% -> 0%
where the time goes in v1:
time: 365 us; the launch traced here: 364 us
  blocking collectives  228 us (62%)
  waiting for transfers between devices  50.7 us (14%)
  Pallas kernels  38.5 us (11%)
  starting transfers between devices  28.6 us (8%)
  local copies, waits for them, and re-layouts  15.4 us (4%)
    all_to_all x6, blocking collectives, over_sensor(): return lax.all_to_all(msg, 'sensor', 0, 0, tiled=True)  134 us
    all_to_all x5, blocking collectives, over_z(): lax.all_to_all(msg, 'basis', 0, 0, tiled=True, axis_index_groups=Z_GROUPS)  77.6 us
    all_to_all x2, waiting for transfers between devices, over_sensor(): return lax.all_to_all(msg, 'sensor', 0, 0, tiled=True)  31.2 us
    psum x1, blocking collectives, per_device(): asqs.append(lax.psum(asq, 'basis'))  16.5 us
    pallas_call x3, Pallas kernels, per_device(): send, keep, asq = forward(core, slots, gathered[-1], tiles)  16.4 us
    unnamed x17, local copies, waits for them, and re-layouts  14.1 us
    all_to_all x1, waiting for transfers between devices, over_z(): lax.all_to_all(msg, 'basis', 0, 0, tiled=True, axis_index_groups=Z_GROUPS)  11.4 us
    pallas_call x3, Pallas kernels, per_device(): msg, = backward(core, slots, own, other, tiles)  10.4 us
  transfers between devices with their start and end apart: 9, of which 9 were waited for; matrix products, arithmetic and copies ran while one was open for 0% of the time, Pallas kernels for 0%

profile of v1, /device:TPU:1, one launch (start us, length us, event | category | flops | bytes accessed | tf_op | source)
XLA Modules:
  0.0 363.9 jit_solution(4328273227805351538)
XLA Ops:
  0.6 0.8 copy.7
  1.4 0.1 reshape.28.slot_ref
  1.5 1.2 fusion.11
  2.7 0.0 copy-start
  2.7 2.8 copy-done
  5.4 3.5 shard_map.58
  8.9 27.2 %all_to_all.70.recv_ref = bf16[32,144,128]{2,1,0:T(8,128)(2,1)S(1)} all-to-all(bf16[32,144,128]{2,1,0:T(8,128)(2,1)S(1)} %shard_map.58), channel_id=1, replica_groups=mesh['sensor'=32,'basis'=8] {'sensor'}, dimensions={0} | all-to-all | bytes 2359296 | tf_op jit(solution)/shard_map/all_to_all | solution.py:231
  36.1 1.2 shard_map.59
  37.4 4.2 %all-to-all-start.1 = ((bf16[32,128,128]{2,1,0:T(8,128)(2,1)}), bf16[32,128,128]{2,1,0:T(8,128)(2,1)S(1)}, u32[]{:S(2)}, u32[]{:S(2)}) async-start(bf16[32,128,128]{2,1,0:T(8,128)(2,1)} %get-tuple-element.33), calls=%async_computation.1 | async-start | bytes 2097152 | tf_op jit(solution)/shard_map/all_to_all | solution.py:231
  41.5 15.8 %all-to-all-done.1.g_ref.g0_ref = bf16[32,128,128]{2,1,0:T(8,128)(2,1)S(1)} async-done(((bf16[32,128,128]{2,1,0:T(8,128)(2,1)}), bf16[32,128,128]{2,1,0:T(8,128)(2,1)S(1)}, u32[]{:S(2)}, u32[]{:S(2)}) %all-to-all-start.1) | async-done | bytes 1048608 | tf_op jit(solution)/shard_map/all_to_all | solution.py:231
  57.4 2.8 copy-done.1
  60.2 5.5 %shard_map.60 = (bf16[1552,128]{1,0:T(8,128)(2,1)S(1)}, f32[1536,128]{1,0:T(8,128)S(1)}, f32[1,128]{1,0:T(1,128)S(1)}) custom-call(s32[1]{0:T(128)} %bitcast.core_ref, s32[6]{0:T(128)S(1)} %reshape.28.slot_ref, bf16[32,128,128]{2,1,0:T(8,128)(2,1)S(1)} %all-to-all-done.1.g_ref.g0_ref, bf16[3,2,1024,512]{3,2,1,0:T(8,128)(2,1)S(1)} %bitcast.10), custom_call_target="tpu_custom_call" | custom-call | tf_op jit(solution)/shard_map/pallas_call | solution.py:244
  65.6 3.1 collective-permute-start
  68.7 1.4 collective-permute-done.recv_ref
  70.1 0.8 shard_map.61
  70.9 7.3 %all-to-all-start.2 = ((bf16[4,400,128]{2,1,0:T(8,128)(2,1)}), bf16[4,400,128]{2,1,0:T(8,128)(2,1)S(1)}, u32[]{:S(2)}, u32[]{:S(2)}) async-start(bf16[4,400,128]{2,1,0:T(8,128)(2,1)} %shard_map.61), calls=%async_computation.2 | async-start | bytes 819200 | tf_op jit(solution)/shard_map/all_to_all | solution.py:234
  78.2 0.9 dynamic-slice_convert_fusion.left_ref
  79.1 11.4 %all-to-all-done.2.recv_ref = bf16[4,400,128]{2,1,0:T(8,128)(2,1)S(1)} async-done(((bf16[4,400,128]{2,1,0:T(8,128)(2,1)}), bf16[4,400,128]{2,1,0:T(8,128)(2,1)S(1)}, u32[]{:S(2)}, u32[]{:S(2)}) %all-to-all-start.2) | async-done | bytes 409632 | tf_op jit(solution)/shard_map/all_to_all | solution.py:234
  90.5 0.1 shard_map.62
  90.6 15.1 %all_to_all.71 = bf16[4,384,128]{2,1,0:T(8,128)(2,1)S(1)} all-to-all(bf16[4,384,128]{2,1,0:T(8,128)(2,1)S(1)} %get-tuple-element.39), channel_id=1, replica_groups={{0,2,4,6},{1,3,5,7},{8,10,12,14},{9,11,13,15},{16,18,20,22},{17,19,21,2..., dimensions={0} | all-to-all | bytes 786432 | tf_op jit(solution)/shard_map/all_to_all | solution.py:234
  105.7 1.9 collective-permute-start.1
  107.5 1.3 collective-permute-done.1.other_ref
  108.9 2.8 copy-done.2
  111.7 3.5 shard_map.63
  115.2 22.7 %all_to_all.72.recv_ref = bf16[32,144,128]{2,1,0:T(8,128)(2,1)S(1)} all-to-all(bf16[32,144,128]{2,1,0:T(8,128)(2,1)S(1)} %shard_map.63), channel_id=1, replica_groups=mesh['sensor'=32,'basis'=8] {'sensor'}, dimensions={0} | all-to-all | bytes 2359296 | tf_op jit(solution)/shard_map/all_to_all | solution.py:231
  137.9 0.3 shard_map.64
  138.1 20.0 %all_to_all.73.g_ref.g1_ref = bf16[32,128,128]{2,1,0:T(8,128)(2,1)S(1)} all-to-all(bf16[32,128,128]{2,1,0:T(8,128)(2,1)S(1)} %get-tuple-element.42), channel_id=1, replica_groups=mesh['sensor'=32,'basis'=8] {'sensor'}, dimensions={0} | all-to-all | bytes 2097152 | tf_op jit(solution)/shard_map/all_to_all | solution.py:231
  158.1 2.8 copy-done.3
  160.9 5.5 %shard_map.65 = (bf16[1552,128]{1,0:T(8,128)(2,1)S(1)}, f32[1536,128]{1,0:T(8,128)S(1)}, f32[1,128]{1,0:T(1,128)S(1)}) custom-call(s32[1]{0:T(128)} %bitcast.core_ref, s32[6]{0:T(128)S(1)} %reshape.28.slot_ref, bf16[32,128,128]{2,1,0:T(8,128)(2,1)S(1)} %all_to_all.73.g_ref.g1_ref, bf16[3,2,1024,512]{3,2,1,0:T(8,128)(2,1)S(1)} %bitcast.12), custom_call_target="tpu_custom_call" | custom-call | tf_op jit(solution)/shard_map/pallas_call | solution.py:244
  166.4 2.9 collective-permute-start.2
  169.3 1.4 collective-permute-done.2.recv_ref
  170.6 0.1 shard_map.66
  170.7 15.5 %all_to_all.74.recv_ref = bf16[4,400,128]{2,1,0:T(8,128)(2,1)S(1)} all-to-all(bf16[4,400,128]{2,1,0:T(8,128)(2,1)S(1)} %shard_map.66), channel_id=1, replica_groups={{0,2,4,6},{1,3,5,7},{8,10,12,14},{9,11,13,15},{16,18,20,22},{17,19,21,2..., dimensions={0} | all-to-all | bytes 819200 | tf_op jit(solution)/shard_map/all_to_all | solution.py:234
  186.2 0.1 shard_map.67
  186.3 15.8 %all_to_all.75 = bf16[4,384,128]{2,1,0:T(8,128)(2,1)S(1)} all-to-all(bf16[4,384,128]{2,1,0:T(8,128)(2,1)S(1)} %get-tuple-element.48), channel_id=1, replica_groups={{0,2,4,6},{1,3,5,7},{8,10,12,14},{9,11,13,15},{16,18,20,22},{17,19,21,2..., dimensions={0} | all-to-all | bytes 786432 | tf_op jit(solution)/shard_map/all_to_all | solution.py:234
  202.1 1.3 collective-permute-start.3
  203.4 1.3 collective-permute-done.3.other_ref
  204.7 0.0 copy-done.4
  204.7 3.5 shard_map.68
  208.2 22.2 %all_to_all.76.recv_ref = bf16[32,144,128]{2,1,0:T(8,128)(2,1)S(1)} all-to-all(bf16[32,144,128]{2,1,0:T(8,128)(2,1)S(1)} %shard_map.68), channel_id=1, replica_groups=mesh['sensor'=32,'basis'=8] {'sensor'}, dimensions={0} | all-to-all | bytes 2359296 | tf_op jit(solution)/shard_map/all_to_all | solution.py:231
  230.4 0.3 shard_map.69
  230.7 20.0 %all_to_all.77.g_ref.g2_ref = bf16[32,128,128]{2,1,0:T(8,128)(2,1)S(1)} all-to-all(bf16[32,128,128]{2,1,0:T(8,128)(2,1)S(1)} %get-tuple-element.51), channel_id=1, replica_groups=mesh['sensor'=32,'basis'=8] {'sensor'}, dimensions={0} | all-to-all | bytes 2097152 | tf_op jit(solution)/shard_map/all_to_all | solution.py:231
  250.7 5.5 %shard_map.70 = (bf16[1552,128]{1,0:T(8,128)(2,1)S(1)}, f32[1536,128]{1,0:T(8,128)S(1)}, f32[1,128]{1,0:T(1,128)S(1)}) custom-call(s32[1]{0:T(128)} %bitcast.core_ref, s32[6]{0:T(128)S(1)} %reshape.28.slot_ref, bf16[32,128,128]{2,1,0:T(8,128)(2,1)S(1)} %all_to_all.77.g_ref.g2_ref, bf16[3,2,1024,512]{3,2,1,0:T(8,128)(2,1)S(1)} %bitcast.14), custom_call_target="tpu_custom_call" | custom-call | tf_op jit(solution)/shard_map/pallas_call | solution.py:244
  256.1 0.0 copy-done.5
  256.1 2.7 collective-permute-start.4
  258.9 1.4 collective-permute-done.4.recv_ref
  260.2 0.1 shard_map.71
  260.3 15.4 %all_to_all.78.recv_ref = bf16[4,400,128]{2,1,0:T(8,128)(2,1)S(1)} all-to-all(bf16[4,400,128]{2,1,0:T(8,128)(2,1)S(1)} %shard_map.71), channel_id=1, replica_groups={{0,2,4,6},{1,3,5,7},{8,10,12,14},{9,11,13,15},{16,18,20,22},{17,19,21,2..., dimensions={0} | all-to-all | bytes 819200 | tf_op jit(solution)/shard_map/all_to_all | solution.py:234
  275.7 0.8 shard_map.72
  276.4 15.8 %all_to_all.79 = bf16[4,384,128]{2,1,0:T(8,128)(2,1)S(1)} all-to-all(bf16[4,384,128]{2,1,0:T(8,128)(2,1)S(1)} %get-tuple-element.57), channel_id=1, replica_groups={{0,2,4,6},{1,3,5,7},{8,10,12,14},{9,11,13,15},{16,18,20,22},{17,19,21,2..., dimensions={0} | all-to-all | bytes 786432 | tf_op jit(solution)/shard_map/all_to_all | solution.py:234
  292.2 1.3 collective-permute-start.5
  293.5 1.3 collective-permute-done.5.other_ref
  294.9 3.5 shard_map.73
  298.3 22.2 %all_to_all.80.recv_ref = bf16[32,144,128]{2,1,0:T(8,128)(2,1)S(1)} all-to-all(bf16[32,144,128]{2,1,0:T(8,128)(2,1)S(1)} %shard_map.73), channel_id=1, replica_groups=mesh['sensor'=32,'basis'=8] {'sensor'}, dimensions={0} | all-to-all | bytes 2359296 | tf_op jit(solution)/shard_map/all_to_all | solution.py:231
  320.6 0.9 shard_map.74
  321.5 1.0 copy-done.7
  322.4 4.0 %all-to-all-start.13 = ((bf16[32,128,128]{2,1,0:T(8,128)(2,1)}), bf16[32,128,128]{2,1,0:T(8,128)(2,1)S(1)}, u32[]{:S(2)}, u32[]{:S(2)}) async-start(bf16[32,128,128]{2,1,0:T(8,128)(2,1)} %copy-done.7), calls=%async_computation.13 | async-start | bytes 2097152 | tf_op jit(solution)/shard_map/all_to_all | solution.py:231
  326.4 0.6 multiply_bitcast_fusion
  327.0 15.3 %all-to-all-done.13.g_ref.g3_ref = bf16[32,128,128]{2,1,0:T(8,128)(2,1)S(1)} async-done(((bf16[32,128,128]{2,1,0:T(8,128)(2,1)}), bf16[32,128,128]{2,1,0:T(8,128)(2,1)S(1)}, u32[]{:S(2)}, u32[]{:S(2)}) %all-to-all-start.13) | async-done | bytes 1048608 | tf_op jit(solution)/shard_map/all_to_all | solution.py:231
  342.4 0.2 shard_map.75
  342.6 16.5 %psum.7 = f32[1,128]{1,0:T(1,128)S(1)} all-reduce(f32[1,128]{1,0:T(1,128)S(1)} %shard_map.75), channel_id=1, replica_groups=mesh['sensor'=32,'basis'=8] {'basis'}, use_global_device_ids=true, to_apply=%region_0.0 | all-reduce | flops 128 | bytes 1024 | tf_op jit(solution)/shard_map/psum | solution.py:256
  359.2 0.0 copy-start.6
  359.2 1.2 copy-done.6
  360.4 3.5 shard_map.76
  (12 shorter events, 0.1 us)
Async XLA Ops:
  2.7 2.8 copy-start
  37.4 20.0 %all-to-all-start.1 = ((bf16[32,128,128]{2,1,0:T(8,128)(2,1)}), bf16[32,128,128]{2,1,0:T(8,128)(2,1)S(1)}, u32[]{:S(2)}, u32[]{:S(2)}) async-start(bf16[32,128,128]{2,1,0:T(8,128)(2,1)} %get-tuple-element.33), calls=%async_computation.1 | async-start | bytes 2097152 | tf_op jit(solution)/shard_map/all_to_all | solution.py:231
  57.4 2.8 copy-start.1
  65.6 4.4 %collective-permute-start = (bf16[1552,128]{1,0:T(8,128)(2,1)S(1)}, bf16[1552,128]{1,0:T(8,128)(2,1)S(1)}, u32[]{:S(2)}, u32[]{:S(2)}) collective-permute-start(bf16[1552,128]{1,0:T(8,128)(2,1)S(1)} %get-tuple-element.35), channel_id=1, source_target_pairs={{0,1},{1,0},{2,3},{3,2},{4,5},{5,4},{6,7},{7,6},{8,9},{9,8},{10,11... | collective-permute-start | bytes 1191944 | tf_op jit(solution)/shard_map/ppermute | solution.py:245
  70.9 19.6 %all-to-all-start.2 = ((bf16[4,400,128]{2,1,0:T(8,128)(2,1)}), bf16[4,400,128]{2,1,0:T(8,128)(2,1)S(1)}, u32[]{:S(2)}, u32[]{:S(2)}) async-start(bf16[4,400,128]{2,1,0:T(8,128)(2,1)} %shard_map.61), calls=%async_computation.2 | async-start | bytes 819200 | tf_op jit(solution)/shard_map/all_to_all | solution.py:234
  105.7 3.2 collective-permute-start.1
  108.9 2.8 copy-start.2
  158.1 2.8 copy-start.3
  160.9 43.8 %copy-start.4 = (bf16[3,1,2,1024,512]{4,3,2,1,0:T(8,128)(2,1)S(1)}, bf16[3,1,2,1024,512]{4,3,2,1,0:T(8,128)(2,1)}, u32[]{:S(2)}) copy-start(bf16[3,1,2,1024,512]{4,3,2,1,0:T(8,128)(2,1)} %param.4) | copy-start | bytes 18874372
  166.4 4.3 %collective-permute-start.2 = (bf16[1552,128]{1,0:T(8,128)(2,1)S(1)}, bf16[1552,128]{1,0:T(8,128)(2,1)S(1)}, u32[]{:S(2)}, u32[]{:S(2)}) collective-permute-start(bf16[1552,128]{1,0:T(8,128)(2,1)S(1)} %get-tuple-element.44), channel_id=1, source_target_pairs={{0,1},{1,0},{2,3},{3,2},{4,5},{5,4},{6,7},{7,6},{8,9},{9,8},{10,11... | collective-permute-start | bytes 1191944 | tf_op jit(solution)/shard_map/ppermute | solution.py:245
  202.1 2.6 collective-permute-start.3
  250.7 5.5 %copy-start.5 = (bf16[32,128,128]{2,1,0:T(8,128)(2,1)}, bf16[32,128,128]{2,1,0:T(8,128)(2,1)S(1)}, u32[]{:S(2)}) copy-start(bf16[32,128,128]{2,1,0:T(8,128)(2,1)S(1)} %all_to_all.77.g_ref.g2_ref) | copy-start | bytes 3145732
  256.1 4.1 %collective-permute-start.4 = (bf16[1552,128]{1,0:T(8,128)(2,1)S(1)}, bf16[1552,128]{1,0:T(8,128)(2,1)S(1)}, u32[]{:S(2)}, u32[]{:S(2)}) collective-permute-start(bf16[1552,128]{1,0:T(8,128)(2,1)S(1)} %get-tuple-element.53), channel_id=1, source_target_pairs={{0,1},{1,0},{2,3},{3,2},{4,5},{5,4},{6,7},{7,6},{8,9},{9,8},{10,11... | collective-permute-start | bytes 1191944 | tf_op jit(solution)/shard_map/ppermute | solution.py:245
  292.2 2.6 collective-permute-start.5
  321.5 1.0 copy-start.7
  322.4 19.9 %all-to-all-start.13 = ((bf16[32,128,128]{2,1,0:T(8,128)(2,1)}), bf16[32,128,128]{2,1,0:T(8,128)(2,1)S(1)}, u32[]{:S(2)}, u32[]{:S(2)}) async-start(bf16[32,128,128]{2,1,0:T(8,128)(2,1)} %copy-done.7), calls=%async_computation.13 | async-start | bytes 2097152 | tf_op jit(solution)/shard_map/all_to_all | solution.py:231
  359.2 1.2 copy-start.6

commit v2 on v1

v2 whole, which is shorter than its diff:
```python
import functools

import jax
import jax.numpy as jnp
from jax import lax
from jax.experimental import pallas as pl
from jax.experimental.pallas import tpu as pltpu
from jax.sharding import PartitionSpec as P

CB_DEV = 8
ITERS = 3
EPS = 1e-06
LANES = 128
EXTRA = 16
TAIL = 8
VMEM_LIMIT = 24 * 1024 * 1024

BF = jnp.bfloat16
F32 = jnp.float32
Z_GROUPS = [[0, 2, 4, 6], [1, 3, 5, 7]]
CORE_PERM = [(i, i ^ 1) for i in range(8)]

VM = pl.BlockSpec(memory_space=pltpu.VMEM)
SM = pl.BlockSpec(memory_space=pltpu.SMEM)
ANY = pl.BlockSpec(memory_space=pl.ANY)


def sds(shape, dtype):
    return jax.ShapeDtypeStruct(shape, dtype)


def call(body, ins, outs, scratch=(), flops=0):
    return pl.pallas_call(
        body,
        in_specs=ins,
        out_specs=[VM] * len(outs),
        out_shape=outs,
        scratch_shapes=scratch,
        compiler_params=pltpu.CompilerParams(vmem_limit_bytes=VMEM_LIMIT),
        cost_estimate=pl.CostEstimate(
            flops=int(flops), bytes_accessed=(4 << 20) if flops else (1 << 20), transcendentals=0
        ),
    )


def pack_row(row, rows=EXTRA):
    high = row.astype(BF).astype(F32)
    low = row - high
    which = lax.broadcasted_iota(jnp.int32, (rows, LANES), 0)
    return jnp.where(which == 0, high, jnp.where(which == 1, low, 0.0))


def unpack_rows(tile):
    wide = tile.astype(F32)
    if wide.ndim == 3:
        wide = jnp.sum(wide, axis=0)
    return jnp.sum(wide, axis=0, keepdims=True)


def across(row):
    return jnp.transpose(jnp.broadcast_to(row, (LANES, LANES)))


def chunk_of(q):
    return lax.div(q, 2), pl.multiple_of(lax.rem(q, 2) * 512, 512)


def products(slot_ref, g_ref, tiles_ref, q):
    seg, top = chunk_of(q)
    acc = None
    for j in range(2):
        base = slot_ref[j, seg] * 4
        operand = jnp.concatenate([g_ref[base + t] for t in range(4)], axis=1)
        part = lax.dot_general(
            tiles_ref[seg, j, pl.ds(top, 512), :],
            operand,
            (((1,), (1,)), ((), ())),
            preferred_element_type=F32,
        )
        acc = part if acc is None else acc + part
    return acc


def squares(g_ref):
    totals = [jnp.zeros((LANES, LANES), F32) for _ in range(2)]
    for q in range(32):
        piece = g_ref[q].astype(F32)
        totals[q % 2] = totals[q % 2] + piece * piece
    return jnp.sum(jnp.transpose(totals[0] + totals[1]), axis=0, keepdims=True)


def send_body(core_ref, slot_ref, g_ref, tiles_ref, send_ref, asq_ref):
    first = 3 * (1 - core_ref[0])
    for i in range(3):
        acc = products(slot_ref, g_ref, tiles_ref, first + i)
        send_ref[i * 512 : (i + 1) * 512, :] = acc.astype(BF)
    asq = squares(g_ref)
    asq_ref[...] = asq
    send_ref[1536:1552, :] = pack_row(asq).astype(BF)


def keep_body(core_ref, slot_ref, g_ref, tiles_ref, keep_ref):
    first = 3 * core_ref[0]
    for i in range(3):
        keep_ref[i * 512 : (i + 1) * 512, :] = products(slot_ref, g_ref, tiles_ref, first + i)


def merge_body(keep_ref, recv_ref, asq_ref, msg_ref):
    tail = pack_row(asq_ref[...] + unpack_rows(recv_ref[1536:1552, :])).astype(BF)
    for z in range(4):
        part = keep_ref[z * 384 : (z + 1) * 384, :] + recv_ref[z * 384 : (z + 1) * 384, :].astype(F32)
        msg_ref[z, 0:384, :] = part.astype(BF)
        msg_ref[z, 384:400, :] = tail


def left_body(recv_ref, left_ref, bsq_ref, new_ref, msg_ref, asq_ref):
    asq = unpack_rows(recv_ref[:, 384:400, :])
    alpha = jnp.sqrt(asq + EPS)
    beta = jnp.sqrt(bsq_ref[...] + EPS)
    total = recv_ref[0, 0:384, :].astype(F32)
    for z in range(1, 4):
        total = total + recv_ref[z, 0:384, :].astype(F32)
    fresh = total * (1.0 / alpha) - (alpha / beta) * left_ref[...].astype(F32)
    new_ref[...] = fresh
    narrow = fresh.astype(BF)
    for z in range(4):
        msg_ref[z] = narrow
    asq_ref[...] = asq


def spread(slot_ref, chunk, tiles_ref, acc, q):
    seg, top = chunk_of(q)
    for j in range(2):
        acc[slot_ref[j, seg]] += lax.dot_general(
            chunk,
            tiles_ref[seg, j, pl.ds(top, 512), :],
            (((0,), (0,)), ((), ())),
            preferred_element_type=F32,
        )


def row_squares(ref):
    total = jnp.zeros((8, LANES), F32)
    for i in range(ref.shape[0] // 512):
        wide = ref[i * 512 : (i + 1) * 512, :].astype(F32)
        total = total + jnp.sum((wide * wide).reshape(64, 8, LANES), axis=0)
    return jnp.sum(total, axis=0, keepdims=True)


def write_pieces(msg_ref, tail, piece):
    for q in range(32):
        lane = (q % 4) * LANES
        msg_ref[q] = jnp.concatenate([piece(q // 4, lane), tail], axis=0).astype(BF)


def back_first_body(
    start_ref, slot_ref, rows_ref, tiles_in, msg_ref, tiles_ref, left_ref, acc, sem
):
    copy = pltpu.make_async_copy(tiles_in, tiles_ref, sem)
    copy.start()
    acc[...] = jnp.zeros_like(acc)
    left_ref[...] = rows_ref[pl.ds(pl.multiple_of(start_ref[0], 128), 384), :].astype(F32)
    tail = pack_row(row_squares(rows_ref), TAIL)
    for seg in range(3):
        for j in range(2):
            acc[slot_ref[j, seg]] += lax.dot_general(
                rows_ref[seg * 1024 : (seg + 1) * 1024, :],
                tiles_in[seg, j],
                (((0,), (0,)), ((), ())),
                preferred_element_type=F32,
            )
    write_pieces(msg_ref, tail, lambda p, lane: acc[p, :, lane : lane + LANES])
    copy.wait()


def back_own_body(core_ref, slot_ref, rows_ref, tiles_ref, acc_ref, bsq_ref):
    first = 3 * core_ref[0]
    acc_ref[...] = jnp.zeros_like(acc_ref)
    for i in range(3):
        spread(slot_ref, rows_ref[i * 512 : (i + 1) * 512, :], tiles_ref, acc_ref, first + i)
    bsq_ref[...] = row_squares(rows_ref)


def back_other_body(core_ref, slot_ref, rows_ref, acc_ref, bsq_ref, tiles_ref, msg_ref, acc):
    first = 3 * (1 - core_ref[0])
    acc[...] = acc_ref[...]
    for i in range(3):
        spread(slot_ref, rows_ref[i * 512 : (i + 1) * 512, :], tiles_ref, acc, first + i)
    tail = pack_row(row_squares(rows_ref) + bsq_ref[...], TAIL)
    write_pieces(msg_ref, tail, lambda p, lane: acc[p, :, lane : lane + LANES])


def share_body(first, recv_ref, *refs):
    if first:
        r_ref, msg_ref, bsq_ref = refs
    else:
        prev_ref, asq_ref, r_ref, msg_ref, bsq_ref = refs
    total = recv_ref[0].astype(F32)
    for q in range(1, 32):
        total = total + recv_ref[q].astype(F32)
    bsq = jnp.sum(total[LANES : LANES + TAIL, :], axis=0, keepdims=True)
    beta = jnp.sqrt(bsq + EPS)
    fresh = total[0:LANES, :] * across(1.0 / beta)
    if not first:
        alpha = jnp.sqrt(asq_ref[...] + EPS)
        fresh = fresh - across(beta / alpha) * prev_ref[...]
    r_ref[...] = fresh
    narrow = fresh.astype(BF)
    for q in range(32):
        msg_ref[q] = narrow
    bsq_ref[...] = bsq


def square_body(g_ref, msg_ref):
    tile = pack_row(squares(g_ref)).astype(BF)
    for i in range(8):
        msg_ref[i] = tile


def coef_body(b0, b1, b2, b3, a0, a1, a2, coef_ref, phi_ref):
    beta = [jnp.sqrt(b[...] + EPS) for b in (b0, b1, b2, b3)]
    alpha = [jnp.sqrt(a[...] + EPS) for a in (a0, a1, a2)]
    phi_bar, rho_bar = beta[0], alpha[0]
    steps, shifts = [], []
    for k in range(ITERS):
        rho = jnp.sqrt(rho_bar * rho_bar + beta[k + 1] * beta[k + 1])
        cosine, sine = rho_bar / rho, beta[k + 1] / rho
        steps.append(cosine * phi_bar / rho)
        phi_bar = sine * phi_bar
        if k < ITERS - 1:
            shifts.append(sine * alpha[k + 1] / rho)
            rho_bar = -cosine * alpha[k + 1]
    s1, s2, s3 = steps
    t1, t2 = shifts
    rows = [
        (s1 - s2 * t1 + s3 * t2 * t1) / alpha[0],
        (s2 - s3 * t2) / alpha[1],
        s3 / alpha[2],
        t2 * t1 / alpha[0],
        -t2 / alpha[1],
        1.0 / alpha[2],
        sine / rho,
        jnp.zeros_like(s1),
    ]
    coef_ref[...] = jnp.concatenate(rows, axis=0)
    phi_ref[...] = phi_bar


def write_out(out_hbm, stage, sems, block):
    copies = []
    for i in range(8):
        rows = pl.ds(i * 512, 512)
        for q in range(4 * i, 4 * i + 4):
            stage[q * 128 : (q + 1) * 128, :] = jnp.transpose(block(q))
        copies.append(pltpu.make_async_copy(stage.at[rows], out_hbm.at[rows], sems.at[i]))
        copies[-1].start()
    for c in copies:
        c.wait()


def solution_body(coef_ref, g0_ref, g1_ref, g2_ref, sol_hbm, stage, sems):
    rows = coef_ref[...]
    wide = [across(rows[i : i + 1, :]) for i in range(3)]

    def block(q):
        out = wide[0] * g0_ref[q].astype(F32)
        out = out + wide[1] * g1_ref[q].astype(F32)
        return out + wide[2] * g2_ref[q].astype(F32)

    write_out(sol_hbm, stage, sems, block)


def search_body(coef_ref, asq_ref, g0_ref, g1_ref, g2_ref, g3_ref, search_hbm, stage, sems):
    rows = coef_ref[...]
    alpha = jnp.sqrt(unpack_rows(asq_ref[...]) + EPS)
    shift = -alpha * rows[6:7, :]
    wide = [across(shift * rows[3 + i : 4 + i, :]) for i in range(3)] + [across(1.0 / alpha)]

    def block(q):
        out = wide[0] * g0_ref[q].astype(F32)
        out = out + wide[1] * g1_ref[q].astype(F32)
        out = out + wide[2] * g2_ref[q].astype(F32)
        return out + wide[3] * g3_ref[q].astype(F32)

    write_out(search_hbm, stage, sems, block)


def combine(body, count):
    return pl.pallas_call(
        body,
        in_specs=[VM] * count,
        out_specs=ANY,
        out_shape=sds((4096, LANES), F32),
        scratch_shapes=[pltpu.VMEM((4096, LANES), F32), pltpu.SemaphoreType.DMA((8,))],
        compiler_params=pltpu.CompilerParams(vmem_limit_bytes=VMEM_LIMIT),
        cost_estimate=pl.CostEstimate(flops=1 << 22, bytes_accessed=4 << 20, transcendentals=0),
    )


def per_device(readings, design_tiles, pattern):
    tiles = design_tiles.reshape(3, 2, 1024, 512)
    slots = jnp.transpose(pattern, (1, 2, 0)).reshape(2, 3)
    basis = lax.axis_index("basis")
    core = lax.rem(basis, 2).reshape(1).astype(jnp.int32)
    z_hi = lax.div(basis, 2)
    acc_type = sds((8, LANES, 512), F32)
    row_type = sds((1, LANES), F32)
    msg_type = sds((32, LANES + TAIL, LANES), BF)
    acc_buf = pltpu.VMEM((8, LANES, 512), F32)

    send_half = call(send_body, [SM, SM, VM, VM], [sds((1552, LANES), BF), row_type], flops=4e8)
    keep_half = call(keep_body, [SM, SM, VM, VM], [sds((1536, LANES), F32)], flops=4e8)
    merge = call(merge_body, [VM] * 3, [sds((4, 400, LANES), BF)])
    left = call(left_body, [VM] * 3, [sds((384, LANES), F32), sds((4, 384, LANES), BF), row_type])
    back_first = call(
        back_first_body,
        [SM, SM, VM, VM],
        [msg_type, sds((3, 2, 1024, 512), BF), sds((384, LANES), F32)],
        [acc_buf, pltpu.SemaphoreType.DMA(())],
        flops=8e8,
    )
    back_own = call(back_own_body, [SM, SM, VM, VM], [acc_type, row_type], flops=4e8)
    back_other = call(back_other_body, [SM, SM, VM, VM, VM, VM], [msg_type], [acc_buf], flops=4e8)
    share_outs = [sds((LANES, LANES), F32), sds((32, LANES, LANES), BF), row_type]
    share_first = call(functools.partial(share_body, True), [VM], share_outs)
    share = call(functools.partial(share_body, False), [VM] * 3, share_outs)

    def over_sensor(msg):
        return lax.all_to_all(msg, "sensor", 0, 0, tiled=True)

    def over_z(msg):
        return lax.all_to_all(msg, "basis", 0, 0, tiled=True, axis_index_groups=Z_GROUPS)

    start = core * 1536 + z_hi.astype(jnp.int32) * 384
    slots, core, start = lax.optimization_barrier((slots, core, start))
    msg, tiles, left_rows = back_first(start, slots, readings, tiles)
    r, msg, bsq = share_first(over_sensor(msg))
    gathered = [over_sensor(msg)]
    bsqs = [bsq]
    asqs = []
    for sweep in range(ITERS):
        send, asq = send_half(core, slots, gathered[-1], tiles)
        other = lax.ppermute(send, "basis", CORE_PERM)
        (keep,) = keep_half(core, slots, gathered[-1], tiles)
        (msg,) = merge(keep, other, asq)
        left_rows, msg, asq = left(over_z(msg), left_rows, bsqs[-1])
        asqs.append(asq)
        own = over_z(msg).reshape(1536, LANES)
        other = lax.ppermute(own, "basis", CORE_PERM)
        acc, own_bsq = back_own(core, slots, own, tiles)
        (msg,) = back_other(core, slots, other, acc, own_bsq, tiles)
        r, msg, bsq = share(over_sensor(msg), r, asq)
        bsqs.append(bsq)
        if sweep == ITERS - 1:
            coefs = call(coef_body, [VM] * 7, [sds((8, LANES), F32), row_type])
            coef, phi_bar = coefs(*bsqs, *asqs)
            sol = combine(solution_body, 4)(coef, *gathered)
            msg, sol, phi_bar = lax.optimization_barrier((msg, sol, phi_bar))
        gathered.append(over_sensor(msg))
    (msg,) = call(square_body, [VM], [sds((8, EXTRA, LANES), BF)])(gathered[-1])
    msg = lax.all_to_all(msg, "basis", 0, 0, tiled=True)
    search = combine(search_body, 6)(coef, msg, *gathered)
    return sol, search, phi_bar.reshape(LANES)


def solution(mesh):
    placed = (P("sensor", None), P("sensor", "basis", None, None, None), P("sensor", "basis", None))
    return jax.shard_map(
        per_device,
        mesh=mesh,
        in_specs=placed,
        out_specs=(P("basis", None), P("basis", None), P()),
        check_vma=False,
    )
```

time: 365 us -> 328 us (0.90)
  blocking collectives: 228 us -> 279 us
  waiting for transfers between devices: 50.7 us -> 0.02 us
  starting transfers between devices: 28.6 us -> 15.1 us
  Pallas kernels: 38.5 us -> 27.1 us
  local copies, waits for them, and re-layouts: 15.4 us -> 4.6 us
    all_to_all x3 -> x0, waiting for transfers between devices: 42.6 us -> none  [the longest x2 31.2 us: over_sensor(): return lax.all_to_all(msg, 'sensor', 0, 0, tiled=True)]
    all_to_all x6 -> x8, blocking collectives: 134 us -> 172 us  [over_sensor(): return lax.all_to_all(msg, 'sensor', 0, 0, tiled=True)]
    all_to_all x5 -> x6, blocking collectives: 77.6 us -> 95.2 us  [over_z(): lax.all_to_all(msg, 'basis', 0, 0, tiled=True, axis_index_groups=Z_GROUPS)]
    psum x1 -> x0, blocking collectives: 16.5 us -> none  [per_device(): asqs.append(lax.psum(asq, 'basis'))]
    all_to_all x3 -> x0, starting transfers between devices: 15.4 us -> none  [the longest x2 8.16 us: over_sensor(): return lax.all_to_all(msg, 'sensor', 0, 0, tiled=True)]
    all_to_all x0 -> x1, blocking collectives: none -> 12.2 us  [per_device(): msg = lax.all_to_all(msg, 'basis', 0, 0, tiled=True)]
    pallas_call x9 -> x17, Pallas kernels: 33.9 us -> 24.3 us  [the longest x3 4.78 us: per_device(): send, asq = send_half(core, slots, gathered[-1], tiles)]
    unnamed x17 -> x8, local copies, waits for them, and re-layouts: 14.1 us -> 4.6 us
  transfers between devices with their start and end apart: 9 -> 6, of which waited for: 9 -> 0; matrix products, arithmetic and copies ran while one was open for 0% -> 0% of each run, Pallas kernels for 0% -> 3%
where the time goes in v2:
time: 328 us; the launch traced here: 327 us
  blocking collectives  279 us (85%)
  Pallas kernels  27.1 us (8%)
  starting transfers between devices  15.1 us (5%)
  local copies, waits for them, and re-layouts  4.6 us (1%)
    all_to_all x8, blocking collectives, over_sensor(): return lax.all_to_all(msg, 'sensor', 0, 0, tiled=True)  172 us
    all_to_all x6, blocking collectives, over_z(): lax.all_to_all(msg, 'basis', 0, 0, tiled=True, axis_index_groups=Z_GROUPS)  95.2 us
    all_to_all x1, blocking collectives, per_device(): msg = lax.all_to_all(msg, 'basis', 0, 0, tiled=True)  12.2 us
    ppermute x3, starting transfers between devices, per_device(): other = lax.ppermute(send, 'basis', CORE_PERM)  8.57 us
  transfers between devices with their start and end apart: 6, of which 0 were waited for; matrix products, arithmetic and copies ran while one was open for 0% of the time, Pallas kernels for 3%

profile of v2, /device:TPU:1, one launch (start us, length us, event | category | flops | bytes accessed | tf_op | source)
XLA Modules:
  0.0 327.0 jit_solution(16246707864114307020)
XLA Ops:
  0.6 0.0 copy-start
  0.6 2.8 copy-done
  3.4 0.0 copy-start.1
  3.4 1.1 copy-done.1
  4.6 0.0 copy-start.2
  4.6 0.7 copy-done.2
  5.2 2.3 shard_map.58
  7.5 26.4 %all_to_all.75.recv_ref = bf16[32,136,128]{2,1,0:T(8,128)(2,1)S(1)} all-to-all(bf16[32,136,128]{2,1,0:T(8,128)(2,1)S(1)} %get-tuple-element.48), channel_id=1, replica_groups=mesh['sensor'=32,'basis'=8] {'sensor'}, dimensions={0} | all-to-all | bytes 2228224 | tf_op jit(solution)/shard_map/all_to_all | solution.py:329
  34.0 0.3 shard_map.59
  34.2 0.0 copy-start.3
  34.2 19.1 %all_to_all.76.g_ref.g0_ref = bf16[32,128,128]{2,1,0:T(8,128)(2,1)S(1)} all-to-all(bf16[32,128,128]{2,1,0:T(8,128)(2,1)S(1)} %get-tuple-element.49), channel_id=1, replica_groups=mesh['sensor'=32,'basis'=8] {'sensor'}, dimensions={0} | all-to-all | bytes 2097152 | tf_op jit(solution)/shard_map/all_to_all | solution.py:329
  53.4 0.0 copy-done.3
  53.4 1.6 shard_map.61
  55.0 3.3 collective-permute-start
  58.3 1.5 shard_map.60.keep_ref
  59.8 0.0 collective-permute-done.recv_ref
  59.8 0.1 shard_map.62
  59.9 19.9 %all_to_all.77.recv_ref = bf16[4,400,128]{2,1,0:T(8,128)(2,1)S(1)} all-to-all(bf16[4,400,128]{2,1,0:T(8,128)(2,1)S(1)} %shard_map.62), channel_id=1, replica_groups={{0,2,4,6},{1,3,5,7},{8,10,12,14},{9,11,13,15},{16,18,20,22},{17,19,21,2..., dimensions={0} | all-to-all | bytes 819200 | tf_op jit(solution)/shard_map/all_to_all | solution.py:332
  79.8 0.1 shard_map.63
  79.9 15.1 %all_to_all.78 = bf16[4,384,128]{2,1,0:T(8,128)(2,1)S(1)} all-to-all(bf16[4,384,128]{2,1,0:T(8,128)(2,1)S(1)} %get-tuple-element.55), channel_id=1, replica_groups={{0,2,4,6},{1,3,5,7},{8,10,12,14},{9,11,13,15},{16,18,20,22},{17,19,21,2..., dimensions={0} | all-to-all | bytes 786432 | tf_op jit(solution)/shard_map/all_to_all | solution.py:332
  95.0 2.0 collective-permute-start.1
  97.0 1.4 shard_map.64
  98.4 0.0 collective-permute-done.1.rows_ref
  98.4 1.4 shard_map.65
  99.8 21.9 %all_to_all.79.recv_ref = bf16[32,136,128]{2,1,0:T(8,128)(2,1)S(1)} all-to-all(bf16[32,136,128]{2,1,0:T(8,128)(2,1)S(1)} %shard_map.65), channel_id=1, replica_groups=mesh['sensor'=32,'basis'=8] {'sensor'}, dimensions={0} | all-to-all | bytes 2228224 | tf_op jit(solution)/shard_map/all_to_all | solution.py:329
  121.8 0.3 shard_map.66
  122.0 20.1 %all_to_all.80.g_ref.g1_ref = bf16[32,128,128]{2,1,0:T(8,128)(2,1)S(1)} all-to-all(bf16[32,128,128]{2,1,0:T(8,128)(2,1)S(1)} %get-tuple-element.60), channel_id=1, replica_groups=mesh['sensor'=32,'basis'=8] {'sensor'}, dimensions={0} | all-to-all | bytes 2097152 | tf_op jit(solution)/shard_map/all_to_all | solution.py:329
  142.1 1.6 shard_map.68
  143.7 2.7 collective-permute-start.2
  146.4 1.5 shard_map.67.keep_ref
  147.9 0.0 collective-permute-done.2.recv_ref
  147.9 0.1 shard_map.69
  148.0 15.3 %all_to_all.81.recv_ref = bf16[4,400,128]{2,1,0:T(8,128)(2,1)S(1)} all-to-all(bf16[4,400,128]{2,1,0:T(8,128)(2,1)S(1)} %shard_map.69), channel_id=1, replica_groups={{0,2,4,6},{1,3,5,7},{8,10,12,14},{9,11,13,15},{16,18,20,22},{17,19,21,2..., dimensions={0} | all-to-all | bytes 819200 | tf_op jit(solution)/shard_map/all_to_all | solution.py:332
  163.3 0.1 shard_map.70
  163.4 15.1 %all_to_all.82 = bf16[4,384,128]{2,1,0:T(8,128)(2,1)S(1)} all-to-all(bf16[4,384,128]{2,1,0:T(8,128)(2,1)S(1)} %get-tuple-element.65), channel_id=1, replica_groups={{0,2,4,6},{1,3,5,7},{8,10,12,14},{9,11,13,15},{16,18,20,22},{17,19,21,2..., dimensions={0} | all-to-all | bytes 786432 | tf_op jit(solution)/shard_map/all_to_all | solution.py:332
  178.5 2.0 collective-permute-start.3
  180.5 1.4 shard_map.71
  181.9 0.0 collective-permute-done.3.rows_ref
  181.9 1.4 shard_map.72
  183.3 21.9 %all_to_all.83.recv_ref = bf16[32,136,128]{2,1,0:T(8,128)(2,1)S(1)} all-to-all(bf16[32,136,128]{2,1,0:T(8,128)(2,1)S(1)} %shard_map.72), channel_id=1, replica_groups=mesh['sensor'=32,'basis'=8] {'sensor'}, dimensions={0} | all-to-all | bytes 2228224 | tf_op jit(solution)/shard_map/all_to_all | solution.py:329
  205.3 0.3 shard_map.73
  205.5 20.1 %all_to_all.84.g_ref.g2_ref = bf16[32,128,128]{2,1,0:T(8,128)(2,1)S(1)} all-to-all(bf16[32,128,128]{2,1,0:T(8,128)(2,1)S(1)} %get-tuple-element.70), channel_id=1, replica_groups=mesh['sensor'=32,'basis'=8] {'sensor'}, dimensions={0} | all-to-all | bytes 2097152 | tf_op jit(solution)/shard_map/all_to_all | solution.py:329
  225.6 1.6 shard_map.75
  227.2 2.7 collective-permute-start.4
  229.9 1.5 shard_map.74.keep_ref
  231.4 0.0 collective-permute-done.4.recv_ref
  231.4 0.1 shard_map.76
  231.5 15.6 %all_to_all.85.recv_ref = bf16[4,400,128]{2,1,0:T(8,128)(2,1)S(1)} all-to-all(bf16[4,400,128]{2,1,0:T(8,128)(2,1)S(1)} %shard_map.76), channel_id=1, replica_groups={{0,2,4,6},{1,3,5,7},{8,10,12,14},{9,11,13,15},{16,18,20,22},{17,19,21,2..., dimensions={0} | all-to-all | bytes 819200 | tf_op jit(solution)/shard_map/all_to_all | solution.py:332
  247.1 0.8 shard_map.77
  247.8 14.3 %all_to_all.86 = bf16[4,384,128]{2,1,0:T(8,128)(2,1)S(1)} all-to-all(bf16[4,384,128]{2,1,0:T(8,128)(2,1)S(1)} %get-tuple-element.75), channel_id=1, replica_groups={{0,2,4,6},{1,3,5,7},{8,10,12,14},{9,11,13,15},{16,18,20,22},{17,19,21,2..., dimensions={0} | all-to-all | bytes 786432 | tf_op jit(solution)/shard_map/all_to_all | solution.py:332
  262.1 2.4 collective-permute-start.5
  264.5 1.4 shard_map.78
  265.9 0.0 collective-permute-done.5.rows_ref
  265.9 1.4 shard_map.79
  267.3 22.1 %all_to_all.87.recv_ref = bf16[32,136,128]{2,1,0:T(8,128)(2,1)S(1)} all-to-all(bf16[32,136,128]{2,1,0:T(8,128)(2,1)S(1)} %shard_map.79), channel_id=1, replica_groups=mesh['sensor'=32,'basis'=8] {'sensor'}, dimensions={0} | all-to-all | bytes 2228224 | tf_op jit(solution)/shard_map/all_to_all | solution.py:329
  289.5 0.9 shard_map.80
  290.3 0.6 shard_map.81
  290.9 1.6 shard_map.82
  292.6 20.1 %all_to_all.88.g_ref.g3_ref = bf16[32,128,128]{2,1,0:T(8,128)(2,1)S(1)} all-to-all(bf16[32,128,128]{2,1,0:T(8,128)(2,1)S(1)} %get-tuple-element.85), channel_id=1, replica_groups=mesh['sensor'=32,'basis'=8] {'sensor'}, dimensions={0} | all-to-all | bytes 2097152 | tf_op jit(solution)/shard_map/all_to_all | solution.py:329
  312.6 0.3 shard_map.83
  312.9 12.2 %all_to_all.89.asq_ref = bf16[8,16,128]{2,1,0:T(8,128)(2,1)S(1)} all-to-all(bf16[8,16,128]{2,1,0:T(8,128)(2,1)S(1)} %shard_map.83), channel_id=1, replica_groups=mesh['sensor'=32,'basis'=8] {'basis'}, dimensions={0} | all-to-all | bytes 65536 | tf_op jit(solution)/shard_map/all_to_all | solution.py:361
  325.1 1.7 shard_map.84
Async XLA Ops:
  0.6 2.8 copy-start
  3.4 1.1 copy-start.1
  4.6 0.7 copy-start.2
  34.2 19.2 %copy-start.3 = (s32[3,1,2]{0,2,1:T(2,128)S(1)}, s32[3,1,2]{0,2,1:T(2,128)}, u32[]{:S(2)}) copy-start(s32[3,1,2]{0,2,1:T(2,128)} %param.5) | copy-start | bytes 76
  55.0 4.8 %collective-permute-start = (bf16[1552,128]{1,0:T(8,128)(2,1)S(1)}, bf16[1552,128]{1,0:T(8,128)(2,1)S(1)}, u32[]{:S(2)}, u32[]{:S(2)}) collective-permute-start(bf16[1552,128]{1,0:T(8,128)(2,1)S(1)} %get-tuple-element.51), channel_id=1, source_target_pairs={{0,1},{1,0},{2,3},{3,2},{4,5},{5,4},{6,7},{7,6},{8,9},{9,8},{10,11... | collective-permute-start | bytes 1191944 | tf_op jit(solution)/shard_map/ppermute | solution.py:343
  95.0 3.4 %collective-permute-start.1 = (bf16[1536,128]{1,0:T(8,128)(2,1)S(1)}, bf16[1536,128]{1,0:T(8,128)(2,1)S(1)}, u32[]{:S(2)}, u32[]{:S(2)}) collective-permute-start(bf16[1536,128]{1,0:T(8,128)(2,1)S(1)} %bitcast.11), channel_id=1, source_target_pairs={{0,1},{1,0},{2,3},{3,2},{4,5},{5,4},{6,7},{7,6},{8,9},{9,8},{10,11... | collective-permute-start | bytes 1179656 | tf_op jit(solution)/shard_map/ppermute | solution.py:349
  143.7 4.2 %collective-permute-start.2 = (bf16[1552,128]{1,0:T(8,128)(2,1)S(1)}, bf16[1552,128]{1,0:T(8,128)(2,1)S(1)}, u32[]{:S(2)}, u32[]{:S(2)}) collective-permute-start(bf16[1552,128]{1,0:T(8,128)(2,1)S(1)} %get-tuple-element.61), channel_id=1, source_target_pairs={{0,1},{1,0},{2,3},{3,2},{4,5},{5,4},{6,7},{7,6},{8,9},{9,8},{10,11... | collective-permute-start | bytes 1191944 | tf_op jit(solution)/shard_map/ppermute | solution.py:343
  178.5 3.4 %collective-permute-start.3 = (bf16[1536,128]{1,0:T(8,128)(2,1)S(1)}, bf16[1536,128]{1,0:T(8,128)(2,1)S(1)}, u32[]{:S(2)}, u32[]{:S(2)}) collective-permute-start(bf16[1536,128]{1,0:T(8,128)(2,1)S(1)} %bitcast.13), channel_id=1, source_target_pairs={{0,1},{1,0},{2,3},{3,2},{4,5},{5,4},{6,7},{7,6},{8,9},{9,8},{10,11... | collective-permute-start | bytes 1179656 | tf_op jit(solution)/shard_map/ppermute | solution.py:349
  227.2 4.2 %collective-permute-start.4 = (bf16[1552,128]{1,0:T(8,128)(2,1)S(1)}, bf16[1552,128]{1,0:T(8,128)(2,1)S(1)}, u32[]{:S(2)}, u32[]{:S(2)}) collective-permute-start(bf16[1552,128]{1,0:T(8,128)(2,1)S(1)} %get-tuple-element.71), channel_id=1, source_target_pairs={{0,1},{1,0},{2,3},{3,2},{4,5},{5,4},{6,7},{7,6},{8,9},{9,8},{10,11... | collective-permute-start | bytes 1191944 | tf_op jit(solution)/shard_map/ppermute | solution.py:343
  262.1 3.8 %collective-permute-start.5 = (bf16[1536,128]{1,0:T(8,128)(2,1)S(1)}, bf16[1536,128]{1,0:T(8,128)(2,1)S(1)}, u32[]{:S(2)}, u32[]{:S(2)}) collective-permute-start(bf16[1536,128]{1,0:T(8,128)(2,1)S(1)} %bitcast.15), channel_id=1, source_target_pairs={{0,1},{1,0},{2,3},{3,2},{4,5},{5,4},{6,7},{7,6},{8,9},{9,8},{10,11... | collective-permute-start | bytes 1179656 | tf_op jit(solution)/shard_map/ppermute | solution.py:349

commit v3 on v2

--- a/solution.py
+++ b/solution.py
@@ -17,7 +17,8 @@
 
 BF = jnp.bfloat16
 F32 = jnp.float32
-Z_GROUPS = [[0, 2, 4, 6], [1, 3, 5, 7]]
+Z_GROUPS = [[6, 4, 2, 0], [7, 5, 3, 1]]
+S_GROUPS = [[(y * 4 + x) * 2 + z for z in range(2) for x in range(4) for y in range(4)]]
 CORE_PERM = [(i, i ^ 1) for i in range(8)]
 
 VM = pl.BlockSpec(memory_space=pltpu.VMEM)
@@ -113,7 +114,7 @@
         msg_ref[z, 384:400, :] = tail
 
 
-def left_body(recv_ref, left_ref, bsq_ref, new_ref, msg_ref, asq_ref):
+def left_body(recv_ref, left_ref, bsq_ref, msg_ref, asq_ref, new_ref=None):
     asq = unpack_rows(recv_ref[:, 384:400, :])
     alpha = jnp.sqrt(asq + EPS)
     beta = jnp.sqrt(bsq_ref[...] + EPS)
@@ -121,7 +122,8 @@
     for z in range(1, 4):
         total = total + recv_ref[z, 0:384, :].astype(F32)
     fresh = total * (1.0 / alpha) - (alpha / beta) * left_ref[...].astype(F32)
-    new_ref[...] = fresh
+    if new_ref is not None:
+        new_ref[...] = fresh
     narrow = fresh.astype(BF)
     for z in range(4):
         msg_ref[z] = narrow
@@ -190,11 +192,11 @@
     write_pieces(msg_ref, tail, lambda p, lane: acc[p, :, lane : lane + LANES])
 
 
-def share_body(first, recv_ref, *refs):
-    if first:
-        r_ref, msg_ref, bsq_ref = refs
-    else:
-        prev_ref, asq_ref, r_ref, msg_ref, bsq_ref = refs
+def share_body(first, last, recv_ref, *refs):
+    if not first:
+        prev_ref, asq_ref = refs[:2]
+        refs = refs[2:]
+    msg_ref, bsq_ref = refs[:2]
     total = recv_ref[0].astype(F32)
     for q in range(1, 32):
         total = total + recv_ref[q].astype(F32)
@@ -204,7 +206,8 @@
     if not first:
         alpha = jnp.sqrt(asq_ref[...] + EPS)
         fresh = fresh - across(beta / alpha) * prev_ref[...]
-    r_ref[...] = fresh
+    if not last:
+        refs[2][...] = fresh
     narrow = fresh.astype(BF)
     for q in range(32):
         msg_ref[q] = narrow
@@ -217,7 +220,7 @@
         msg_ref[i] = tile
 
 
-def coef_body(b0, b1, b2, b3, a0, a1, a2, coef_ref, phi_ref):
+def coefficients(b0, b1, b2, b3, a0, a1, a2):
     beta = [jnp.sqrt(b[...] + EPS) for b in (b0, b1, b2, b3)]
     alpha = [jnp.sqrt(a[...] + EPS) for a in (a0, a1, a2)]
     phi_bar, rho_bar = beta[0], alpha[0]
@@ -242,8 +245,7 @@
         sine / rho,
         jnp.zeros_like(s1),
     ]
-    coef_ref[...] = jnp.concatenate(rows, axis=0)
-    phi_ref[...] = phi_bar
+    return jnp.concatenate(rows, axis=0), phi_bar
 
 
 def write_out(out_hbm, stage, sems, block):
@@ -258,8 +260,11 @@
         c.wait()
 
 
-def solution_body(coef_ref, g0_ref, g1_ref, g2_ref, sol_hbm, stage, sems):
-    rows = coef_ref[...]
+def solution_body(*refs):
+    g0_ref, g1_ref, g2_ref, sol_hbm, coef_ref, phi_ref, stage, sems = refs[7:]
+    rows, phi_bar = coefficients(*refs[:7])
+    coef_ref[...] = rows
+    phi_ref[...] = phi_bar
     wide = [across(rows[i : i + 1, :]) for i in range(3)]
 
     def block(q):
@@ -285,12 +290,12 @@
     write_out(search_hbm, stage, sems, block)
 
 
-def combine(body, count):
+def combine(body, count, smalls=()):
     return pl.pallas_call(
         body,
         in_specs=[VM] * count,
-        out_specs=ANY,
-        out_shape=sds((4096, LANES), F32),
+        out_specs=[ANY] + [VM] * len(smalls),
+        out_shape=[sds((4096, LANES), F32)] + list(smalls),
         scratch_shapes=[pltpu.VMEM((4096, LANES), F32), pltpu.SemaphoreType.DMA((8,))],
         compiler_params=pltpu.CompilerParams(vmem_limit_bytes=VMEM_LIMIT),
         cost_estimate=pl.CostEstimate(flops=1 << 22, bytes_accessed=4 << 20, transcendentals=0),
@@ -311,7 +316,9 @@
     send_half = call(send_body, [SM, SM, VM, VM], [sds((1552, LANES), BF), row_type], flops=4e8)
     keep_half = call(keep_body, [SM, SM, VM, VM], [sds((1536, LANES), F32)], flops=4e8)
     merge = call(merge_body, [VM] * 3, [sds((4, 400, LANES), BF)])
-    left = call(left_body, [VM] * 3, [sds((384, LANES), F32), sds((4, 384, LANES), BF), row_type])
+    left_outs = [sds((4, 384, LANES), BF), row_type, sds((384, LANES), F32)]
+    left = call(left_body, [VM] * 3, left_outs)
+    left_last = call(left_body, [VM] * 3, left_outs[:2])
     back_first = call(
         back_first_body,
         [SM, SM, VM, VM],
@@ -321,45 +328,53 @@
     )
     back_own = call(back_own_body, [SM, SM, VM, VM], [acc_type, row_type], flops=4e8)
     back_other = call(back_other_body, [SM, SM, VM, VM, VM, VM], [msg_type], [acc_buf], flops=4e8)
-    share_outs = [sds((LANES, LANES), F32), sds((32, LANES, LANES), BF), row_type]
-    share_first = call(functools.partial(share_body, True), [VM], share_outs)
-    share = call(functools.partial(share_body, False), [VM] * 3, share_outs)
+    share_outs = [sds((32, LANES, LANES), BF), row_type, sds((LANES, LANES), F32)]
+    share_first = call(functools.partial(share_body, True, False), [VM], share_outs)
+    share = call(functools.partial(share_body, False, False), [VM] * 3, share_outs)
+    share_last = call(functools.partial(share_body, False, True), [VM] * 3, share_outs[:2])
+
+    solve = combine(solution_body, 10, [sds((8, LANES), F32), row_type])
 
     def over_sensor(msg):
-        return lax.all_to_all(msg, "sensor", 0, 0, tiled=True)
+        return lax.all_to_all(msg, "sensor", 0, 0, tiled=True, axis_index_groups=S_GROUPS)
 
     def over_z(msg):
         return lax.all_to_all(msg, "basis", 0, 0, tiled=True, axis_index_groups=Z_GROUPS)
 
-    start = core * 1536 + z_hi.astype(jnp.int32) * 384
+    start = core * 1536 + (3 - z_hi.astype(jnp.int32)) * 384
     slots, core, start = lax.optimization_barrier((slots, core, start))
     msg, tiles, left_rows = back_first(start, slots, readings, tiles)
-    r, msg, bsq = share_first(over_sensor(msg))
+    msg, bsq, r = share_first(over_sensor(msg))
     gathered = [over_sensor(msg)]
     bsqs = [bsq]
     asqs = []
     for sweep in range(ITERS):
+        last = sweep == ITERS - 1
         send, asq = send_half(core, slots, gathered[-1], tiles)
         other = lax.ppermute(send, "basis", CORE_PERM)
         (keep,) = keep_half(core, slots, gathered[-1], tiles)
         (msg,) = merge(keep, other, asq)
-        left_rows, msg, asq = left(over_z(msg), left_rows, bsqs[-1])
+        if last:
+            msg, asq = left_last(over_z(msg), left_rows, bsqs[-1])
+        else:
+            msg, asq, left_rows = left(over_z(msg), left_rows, bsqs[-1])
         asqs.append(asq)
         own = over_z(msg).reshape(1536, LANES)
         other = lax.ppermute(own, "basis", CORE_PERM)
         acc, own_bsq = back_own(core, slots, own, tiles)
         (msg,) = back_other(core, slots, other, acc, own_bsq, tiles)
-        r, msg, bsq = share(over_sensor(msg), r, asq)
+        if last:
+            msg, bsq = share_last(over_sensor(msg), r, asq)
+        else:
+            msg, bsq, r = share(over_sensor(msg), r, asq)
         bsqs.append(bsq)
-        if sweep == ITERS - 1:
-            coefs = call(coef_body, [VM] * 7, [sds((8, LANES), F32), row_type])
-            coef, phi_bar = coefs(*bsqs, *asqs)
-            sol = combine(solution_body, 4)(coef, *gathered)
+        if last:
+            sol, coef, phi_bar = solve(*bsqs, *asqs, *gathered)
             msg, sol, phi_bar = lax.optimization_barrier((msg, sol, phi_bar))
         gathered.append(over_sensor(msg))
     (msg,) = call(square_body, [VM], [sds((8, EXTRA, LANES), BF)])(gathered[-1])
     msg = lax.all_to_all(msg, "basis", 0, 0, tiled=True)
-    search = combine(search_body, 6)(coef, msg, *gathered)
+    (search,) = combine(search_body, 6)(coef, msg, *gathered)
     return sol, search, phi_bar.reshape(LANES)
 
 

time: 328 us -> 324 us (0.988)
  blocking collectives: 279 us -> 259 us
  starting transfers between devices: 15.1 us -> 33 us
    ppermute x3, starting transfers between devices: 6.5 us -> 23.6 us  [per_device(): other = lax.ppermute(own, 'basis', CORE_PERM)]
    all_to_all x6, blocking collectives: 95.2 us -> 80.2 us  [over_z(): lax.all_to_all(msg, 'basis', 0, 0, tiled=True, axis_index_groups=Z_GROUPS)]
    all_to_all x8, blocking collectives: 172 us -> 163 us  [over_sensor(): lax.all_to_all(msg, 'sensor', 0, 0, tiled=True, axis_index_groups=S_GROUPS)]
    all_to_all x1, blocking collectives: 12.2 us -> 15.7 us  [per_device(): msg = lax.all_to_all(msg, 'basis', 0, 0, tiled=True)]
where the time goes in v3:
time: 324 us; the launch traced here: 323 us
  blocking collectives  259 us (80%)
  starting transfers between devices  33 us (10%)
  Pallas kernels  25.8 us (8%)
  local copies, waits for them, and re-layouts  4.6 us (1%)
    all_to_all x8, blocking collectives, over_sensor(): lax.all_to_all(msg, 'sensor', 0, 0, tiled=True, axis_index_groups=S_GROUPS)  163 us
    all_to_all x6, blocking collectives, over_z(): lax.all_to_all(msg, 'basis', 0, 0, tiled=True, axis_index_groups=Z_GROUPS)  80.2 us
    ppermute x3, starting transfers between devices, per_device(): other = lax.ppermute(own, 'basis', CORE_PERM)  23.6 us
    all_to_all x1, blocking collectives, per_device(): msg = lax.all_to_all(msg, 'basis', 0, 0, tiled=True)  15.7 us
    ppermute x3, starting transfers between devices, per_device(): other = lax.ppermute(send, 'basis', CORE_PERM)  9.4 us
  transfers between devices with their start and end apart: 6, of which 0 were waited for; matrix products, arithmetic and copies ran while one was open for 0% of the time, Pallas kernels for 3%

profile of v3, /device:TPU:1, one launch (start us, length us, event | category | flops | bytes accessed | tf_op | source)
XLA Modules:
  0.0 323.5 jit_solution(6134151447859731281)
XLA Ops:
  0.6 0.0 copy-start
  0.6 2.8 copy-done
  3.4 0.0 copy-start.1
  3.4 1.1 copy-done.1
  4.6 0.0 copy-start.2
  4.6 0.7 copy-done.2
  5.2 2.3 shard_map.58
  7.5 26.2 %all_to_all.75.recv_ref = bf16[32,136,128]{2,1,0:T(8,128)(2,1)S(1)} all-to-all(bf16[32,136,128]{2,1,0:T(8,128)(2,1)S(1)} %get-tuple-element.49), channel_id=1, replica_groups={{0,64,128,192,16,80,144,208,32,96,160,224,48,112,176,240,8,72,136,200,2..., dimensions={0} | all-to-all | bytes 2228224 | tf_op jit(solution)/shard_map/all_to_all | solution.py:339
  33.8 0.3 shard_map.59
  34.0 0.0 copy-start.3
  34.0 18.6 %all_to_all.76.g_ref.refs_7_.g0_ref = bf16[32,128,128]{2,1,0:T(8,128)(2,1)S(1)} all-to-all(bf16[32,128,128]{2,1,0:T(8,128)(2,1)S(1)} %get-tuple-element.50), channel_id=1, replica_groups={{0,64,128,192,16,80,144,208,32,96,160,224,48,112,176,240,8,72,136,200,2..., dimensions={0} | all-to-all | bytes 2097152 | tf_op jit(solution)/shard_map/all_to_all | solution.py:339
  52.6 0.0 copy-done.3
  52.6 1.6 shard_map.61
  54.2 3.2 collective-permute-start
  57.4 1.5 shard_map.60.keep_ref
  58.9 0.0 collective-permute-done.recv_ref
  59.0 0.1 shard_map.62
  59.0 15.0 %all_to_all.77.recv_ref = bf16[4,400,128]{2,1,0:T(8,128)(2,1)S(1)} all-to-all(bf16[4,400,128]{2,1,0:T(8,128)(2,1)S(1)} %shard_map.62), channel_id=1, replica_groups={{6,4,2,0},{7,5,3,1},{14,12,10,8},{15,13,11,9},{22,20,18,16},{23,21,19,1..., dimensions={0} | all-to-all | bytes 819200 | tf_op jit(solution)/shard_map/all_to_all | solution.py:342
  74.1 0.1 shard_map.63
  74.2 13.1 %all_to_all.78 = bf16[4,384,128]{2,1,0:T(8,128)(2,1)S(1)} all-to-all(bf16[4,384,128]{2,1,0:T(8,128)(2,1)S(1)} %get-tuple-element.56), channel_id=1, replica_groups={{6,4,2,0},{7,5,3,1},{14,12,10,8},{15,13,11,9},{22,20,18,16},{23,21,19,1..., dimensions={0} | all-to-all | bytes 786432 | tf_op jit(solution)/shard_map/all_to_all | solution.py:342
  87.3 7.8 %collective-permute-start.1 = (bf16[1536,128]{1,0:T(8,128)(2,1)S(1)}, bf16[1536,128]{1,0:T(8,128)(2,1)S(1)}, u32[]{:S(2)}, u32[]{:S(2)}) collective-permute-start(bf16[1536,128]{1,0:T(8,128)(2,1)S(1)} %bitcast.11), channel_id=1, source_target_pairs={{0,1},{1,0},{2,3},{3,2},{4,5},{5,4},{6,7},{7,6},{8,9},{9,8},{10,11... | collective-permute-start | bytes 1179656 | tf_op jit(solution)/shard_map/ppermute | solution.py:363
  95.1 1.4 shard_map.64
  96.5 0.0 collective-permute-done.1.rows_ref
  96.5 1.4 shard_map.65
  97.9 21.2 %all_to_all.79.recv_ref = bf16[32,136,128]{2,1,0:T(8,128)(2,1)S(1)} all-to-all(bf16[32,136,128]{2,1,0:T(8,128)(2,1)S(1)} %shard_map.65), channel_id=1, replica_groups={{0,64,128,192,16,80,144,208,32,96,160,224,48,112,176,240,8,72,136,200,2..., dimensions={0} | all-to-all | bytes 2228224 | tf_op jit(solution)/shard_map/all_to_all | solution.py:339
  119.1 0.3 shard_map.66
  119.4 18.4 %all_to_all.80.g_ref.refs_8_.g1_ref = bf16[32,128,128]{2,1,0:T(8,128)(2,1)S(1)} all-to-all(bf16[32,128,128]{2,1,0:T(8,128)(2,1)S(1)} %get-tuple-element.61), channel_id=1, replica_groups={{0,64,128,192,16,80,144,208,32,96,160,224,48,112,176,240,8,72,136,200,2..., dimensions={0} | all-to-all | bytes 2097152 | tf_op jit(solution)/shard_map/all_to_all | solution.py:339
  137.8 1.6 shard_map.68
  139.4 3.1 collective-permute-start.2
  142.5 1.5 shard_map.67.keep_ref
  144.0 0.0 collective-permute-done.2.recv_ref
  144.1 0.1 shard_map.69
  144.1 13.0 %all_to_all.81.recv_ref = bf16[4,400,128]{2,1,0:T(8,128)(2,1)S(1)} all-to-all(bf16[4,400,128]{2,1,0:T(8,128)(2,1)S(1)} %shard_map.69), channel_id=1, replica_groups={{6,4,2,0},{7,5,3,1},{14,12,10,8},{15,13,11,9},{22,20,18,16},{23,21,19,1..., dimensions={0} | all-to-all | bytes 819200 | tf_op jit(solution)/shard_map/all_to_all | solution.py:342
  157.1 0.1 shard_map.70
  157.2 13.0 %all_to_all.82 = bf16[4,384,128]{2,1,0:T(8,128)(2,1)S(1)} all-to-all(bf16[4,384,128]{2,1,0:T(8,128)(2,1)S(1)} %get-tuple-element.66), channel_id=1, replica_groups={{6,4,2,0},{7,5,3,1},{14,12,10,8},{15,13,11,9},{22,20,18,16},{23,21,19,1..., dimensions={0} | all-to-all | bytes 786432 | tf_op jit(solution)/shard_map/all_to_all | solution.py:342
  170.2 7.9 %collective-permute-start.3 = (bf16[1536,128]{1,0:T(8,128)(2,1)S(1)}, bf16[1536,128]{1,0:T(8,128)(2,1)S(1)}, u32[]{:S(2)}, u32[]{:S(2)}) collective-permute-start(bf16[1536,128]{1,0:T(8,128)(2,1)S(1)} %bitcast.13), channel_id=1, source_target_pairs={{0,1},{1,0},{2,3},{3,2},{4,5},{5,4},{6,7},{7,6},{8,9},{9,8},{10,11... | collective-permute-start | bytes 1179656 | tf_op jit(solution)/shard_map/ppermute | solution.py:363
  178.1 1.4 shard_map.71
  179.4 0.0 collective-permute-done.3.rows_ref
  179.5 1.5 shard_map.72
  180.9 21.0 %all_to_all.83.recv_ref = bf16[32,136,128]{2,1,0:T(8,128)(2,1)S(1)} all-to-all(bf16[32,136,128]{2,1,0:T(8,128)(2,1)S(1)} %shard_map.72), channel_id=1, replica_groups={{0,64,128,192,16,80,144,208,32,96,160,224,48,112,176,240,8,72,136,200,2..., dimensions={0} | all-to-all | bytes 2228224 | tf_op jit(solution)/shard_map/all_to_all | solution.py:339
  201.9 0.3 shard_map.73
  202.1 18.4 %all_to_all.84.g_ref.refs_9_.g2_ref = bf16[32,128,128]{2,1,0:T(8,128)(2,1)S(1)} all-to-all(bf16[32,128,128]{2,1,0:T(8,128)(2,1)S(1)} %get-tuple-element.71), channel_id=1, replica_groups={{0,64,128,192,16,80,144,208,32,96,160,224,48,112,176,240,8,72,136,200,2..., dimensions={0} | all-to-all | bytes 2097152 | tf_op jit(solution)/shard_map/all_to_all | solution.py:339
  220.5 1.6 shard_map.75
  222.1 3.1 collective-permute-start.4
  225.2 1.5 shard_map.74.keep_ref
  226.8 0.0 collective-permute-done.4.recv_ref
  226.8 0.1 shard_map.76
  226.9 13.1 %all_to_all.85.recv_ref = bf16[4,400,128]{2,1,0:T(8,128)(2,1)S(1)} all-to-all(bf16[4,400,128]{2,1,0:T(8,128)(2,1)S(1)} %shard_map.76), channel_id=1, replica_groups={{6,4,2,0},{7,5,3,1},{14,12,10,8},{15,13,11,9},{22,20,18,16},{23,21,19,1..., dimensions={0} | all-to-all | bytes 819200 | tf_op jit(solution)/shard_map/all_to_all | solution.py:342
  240.0 0.1 shard_map.77
  240.0 13.0 %all_to_all.86 = bf16[4,384,128]{2,1,0:T(8,128)(2,1)S(1)} all-to-all(bf16[4,384,128]{2,1,0:T(8,128)(2,1)S(1)} %get-tuple-element.76), channel_id=1, replica_groups={{6,4,2,0},{7,5,3,1},{14,12,10,8},{15,13,11,9},{22,20,18,16},{23,21,19,1..., dimensions={0} | all-to-all | bytes 786432 | tf_op jit(solution)/shard_map/all_to_all | solution.py:342
  253.1 7.9 %collective-permute-start.5 = (bf16[1536,128]{1,0:T(8,128)(2,1)S(1)}, bf16[1536,128]{1,0:T(8,128)(2,1)S(1)}, u32[]{:S(2)}, u32[]{:S(2)}) collective-permute-start(bf16[1536,128]{1,0:T(8,128)(2,1)S(1)} %bitcast.15), channel_id=1, source_target_pairs={{0,1},{1,0},{2,3},{3,2},{4,5},{5,4},{6,7},{7,6},{8,9},{9,8},{10,11... | collective-permute-start | bytes 1179656 | tf_op jit(solution)/shard_map/ppermute | solution.py:363
  261.0 1.4 shard_map.78
  262.3 0.0 collective-permute-done.5.rows_ref
  262.3 1.5 shard_map.79
  263.8 20.9 %all_to_all.87.recv_ref = bf16[32,136,128]{2,1,0:T(8,128)(2,1)S(1)} all-to-all(bf16[32,136,128]{2,1,0:T(8,128)(2,1)S(1)} %shard_map.79), channel_id=1, replica_groups={{0,64,128,192,16,80,144,208,32,96,160,224,48,112,176,240,8,72,136,200,2..., dimensions={0} | all-to-all | bytes 2228224 | tf_op jit(solution)/shard_map/all_to_all | solution.py:339
  284.7 0.3 shard_map.80
  285.0 2.2 shard_map.81
  287.2 18.4 %all_to_all.88.g_ref.g3_ref = bf16[32,128,128]{2,1,0:T(8,128)(2,1)S(1)} all-to-all(bf16[32,128,128]{2,1,0:T(8,128)(2,1)S(1)} %get-tuple-element.87), channel_id=1, replica_groups={{0,64,128,192,16,80,144,208,32,96,160,224,48,112,176,240,8,72,136,200,2..., dimensions={0} | all-to-all | bytes 2097152 | tf_op jit(solution)/shard_map/all_to_all | solution.py:339
  305.6 0.3 shard_map.82
  305.9 15.7 %all_to_all.89.asq_ref = bf16[8,16,128]{2,1,0:T(8,128)(2,1)S(1)} all-to-all(bf16[8,16,128]{2,1,0:T(8,128)(2,1)S(1)} %shard_map.82), channel_id=1, replica_groups=mesh['sensor'=32,'basis'=8] {'basis'}, dimensions={0} | all-to-all | bytes 65536 | tf_op jit(solution)/shard_map/all_to_all | solution.py:376
  321.6 1.7 shard_map.83
Async XLA Ops:
  0.6 2.8 copy-start
  3.4 1.1 copy-start.1
  4.6 0.7 copy-start.2
  34.0 18.6 %copy-start.3 = (s32[3,1,2]{0,2,1:T(2,128)S(1)}, s32[3,1,2]{0,2,1:T(2,128)}, u32[]{:S(2)}) copy-start(s32[3,1,2]{0,2,1:T(2,128)} %param.5) | copy-start | bytes 76
  54.2 4.7 %collective-permute-start = (bf16[1552,128]{1,0:T(8,128)(2,1)S(1)}, bf16[1552,128]{1,0:T(8,128)(2,1)S(1)}, u32[]{:S(2)}, u32[]{:S(2)}) collective-permute-start(bf16[1552,128]{1,0:T(8,128)(2,1)S(1)} %get-tuple-element.52), channel_id=1, source_target_pairs={{0,1},{1,0},{2,3},{3,2},{4,5},{5,4},{6,7},{7,6},{8,9},{9,8},{10,11... | collective-permute-start | bytes 1191944 | tf_op jit(solution)/shard_map/ppermute | solution.py:354
  87.3 9.2 %collective-permute-start.1 = (bf16[1536,128]{1,0:T(8,128)(2,1)S(1)}, bf16[1536,128]{1,0:T(8,128)(2,1)S(1)}, u32[]{:S(2)}, u32[]{:S(2)}) collective-permute-start(bf16[1536,128]{1,0:T(8,128)(2,1)S(1)} %bitcast.11), channel_id=1, source_target_pairs={{0,1},{1,0},{2,3},{3,2},{4,5},{5,4},{6,7},{7,6},{8,9},{9,8},{10,11... | collective-permute-start | bytes 1179656 | tf_op jit(solution)/shard_map/ppermute | solution.py:363
  139.4 4.7 %collective-permute-start.2 = (bf16[1552,128]{1,0:T(8,128)(2,1)S(1)}, bf16[1552,128]{1,0:T(8,128)(2,1)S(1)}, u32[]{:S(2)}, u32[]{:S(2)}) collective-permute-start(bf16[1552,128]{1,0:T(8,128)(2,1)S(1)} %get-tuple-element.62), channel_id=1, source_target_pairs={{0,1},{1,0},{2,3},{3,2},{4,5},{5,4},{6,7},{7,6},{8,9},{9,8},{10,11... | collective-permute-start | bytes 1191944 | tf_op jit(solution)/shard_map/ppermute | solution.py:354
  170.2 9.3 %collective-permute-start.3 = (bf16[1536,128]{1,0:T(8,128)(2,1)S(1)}, bf16[1536,128]{1,0:T(8,128)(2,1)S(1)}, u32[]{:S(2)}, u32[]{:S(2)}) collective-permute-start(bf16[1536,128]{1,0:T(8,128)(2,1)S(1)} %bitcast.13), channel_id=1, source_target_pairs={{0,1},{1,0},{2,3},{3,2},{4,5},{5,4},{6,7},{7,6},{8,9},{9,8},{10,11... | collective-permute-start | bytes 1179656 | tf_op jit(solution)/shard_map/ppermute | solution.py:363
  222.1 4.7 %collective-permute-start.4 = (bf16[1552,128]{1,0:T(8,128)(2,1)S(1)}, bf16[1552,128]{1,0:T(8,128)(2,1)S(1)}, u32[]{:S(2)}, u32[]{:S(2)}) collective-permute-start(bf16[1552,128]{1,0:T(8,128)(2,1)S(1)} %get-tuple-element.72), channel_id=1, source_target_pairs={{0,1},{1,0},{2,3},{3,2},{4,5},{5,4},{6,7},{7,6},{8,9},{9,8},{10,11... | collective-permute-start | bytes 1191944 | tf_op jit(solution)/shard_map/ppermute | solution.py:354
  253.1 9.3 %collective-permute-start.5 = (bf16[1536,128]{1,0:T(8,128)(2,1)S(1)}, bf16[1536,128]{1,0:T(8,128)(2,1)S(1)}, u32[]{:S(2)}, u32[]{:S(2)}) collective-permute-start(bf16[1536,128]{1,0:T(8,128)(2,1)S(1)} %bitcast.15), channel_id=1, source_target_pairs={{0,1},{1,0},{2,3},{3,2},{4,5},{5,4},{6,7},{7,6},{8,9},{9,8},{10,11... | collective-permute-start | bytes 1179656 | tf_op jit(solution)/shard_map/ppermute | solution.py:363

commit v4 on v3

--- a/solution.py
+++ b/solution.py
@@ -18,7 +18,7 @@
 BF = jnp.bfloat16
 F32 = jnp.float32
 Z_GROUPS = [[6, 4, 2, 0], [7, 5, 3, 1]]
-S_GROUPS = [[(y * 4 + x) * 2 + z for z in range(2) for x in range(4) for y in range(4)]]
+S_GROUPS = [[(y * 4 + x) * 2 + z for z in range(2) for x in range(4) for y in (3, 2, 1, 0)]]
 CORE_PERM = [(i, i ^ 1) for i in range(8)]
 
 VM = pl.BlockSpec(memory_space=pltpu.VMEM)
@@ -62,48 +62,46 @@
     return jnp.transpose(jnp.broadcast_to(row, (LANES, LANES)))
 
 
-def chunk_of(q):
-    return lax.div(q, 2), pl.multiple_of(lax.rem(q, 2) * 512, 512)
-
-
-def products(slot_ref, g_ref, tiles_ref, q):
-    seg, top = chunk_of(q)
+def parts_of(half):
+    middle = pl.multiple_of(half * 512, 512)
+    return (
+        (2 * half, 0, 1024, middle),
+        (1, middle, 512, pl.multiple_of((1 - half) * 1024, 512)),
+    )
+
+
+def products(slot_ref, g_ref, tiles_ref, seg, top, rows):
     acc = None
     for j in range(2):
-        base = slot_ref[j, seg] * 4
-        operand = jnp.concatenate([g_ref[base + t] for t in range(4)], axis=1)
-        part = lax.dot_general(
-            tiles_ref[seg, j, pl.ds(top, 512), :],
-            operand,
-            (((1,), (1,)), ((), ())),
+        part = jnp.dot(
+            tiles_ref[seg, j, pl.ds(top, rows), :],
+            g_ref[slot_ref[j, seg]],
             preferred_element_type=F32,
         )
         acc = part if acc is None else acc + part
     return acc
 
 
-def squares(g_ref):
-    totals = [jnp.zeros((LANES, LANES), F32) for _ in range(2)]
-    for q in range(32):
-        piece = g_ref[q].astype(F32)
-        totals[q % 2] = totals[q % 2] + piece * piece
-    return jnp.sum(jnp.transpose(totals[0] + totals[1]), axis=0, keepdims=True)
+def column_squares(g_ref):
+    total = jnp.zeros((8, LANES), F32)
+    for p in range(8):
+        wide = g_ref[p].astype(F32)
+        total = total + jnp.sum((wide * wide).reshape(64, 8, LANES), axis=0)
+    return jnp.sum(total, axis=0, keepdims=True)
 
 
 def send_body(core_ref, slot_ref, g_ref, tiles_ref, send_ref, asq_ref):
-    first = 3 * (1 - core_ref[0])
-    for i in range(3):
-        acc = products(slot_ref, g_ref, tiles_ref, first + i)
-        send_ref[i * 512 : (i + 1) * 512, :] = acc.astype(BF)
-    asq = squares(g_ref)
+    for seg, top, rows, at in parts_of(1 - core_ref[0]):
+        acc = products(slot_ref, g_ref, tiles_ref, seg, top, rows)
+        send_ref[pl.ds(at, rows), :] = acc.astype(BF)
+    asq = column_squares(g_ref)
     asq_ref[...] = asq
     send_ref[1536:1552, :] = pack_row(asq).astype(BF)
 
 
 def keep_body(core_ref, slot_ref, g_ref, tiles_ref, keep_ref):
-    first = 3 * core_ref[0]
-    for i in range(3):
-        keep_ref[i * 512 : (i + 1) * 512, :] = products(slot_ref, g_ref, tiles_ref, first + i)
+    for seg, top, rows, at in parts_of(core_ref[0]):
+        keep_ref[pl.ds(at, rows), :] = products(slot_ref, g_ref, tiles_ref, seg, top, rows)
 
 
 def merge_body(keep_ref, recv_ref, asq_ref, msg_ref):
@@ -130,15 +128,16 @@
     asq_ref[...] = asq
 
 
-def spread(slot_ref, chunk, tiles_ref, acc, q):
-    seg, top = chunk_of(q)
-    for j in range(2):
-        acc[slot_ref[j, seg]] += lax.dot_general(
-            chunk,
-            tiles_ref[seg, j, pl.ds(top, 512), :],
-            (((0,), (0,)), ((), ())),
-            preferred_element_type=F32,
-        )
+def spread(slot_ref, rows_ref, tiles_ref, acc, half):
+    for seg, top, rows, at in parts_of(half):
+        chunk = rows_ref[pl.ds(at, rows), :]
+        for j in range(2):
+            acc[slot_ref[j, seg]] += lax.dot_general(
+                chunk,
+                tiles_ref[seg, j, pl.ds(top, rows), :],
+                (((0,), (0,)), ((), ())),
+                preferred_element_type=F32,
+            )
 
 
 def row_squares(ref):
@@ -176,18 +175,14 @@
 
 
 def back_own_body(core_ref, slot_ref, rows_ref, tiles_ref, acc_ref, bsq_ref):
-    first = 3 * core_ref[0]
     acc_ref[...] = jnp.zeros_like(acc_ref)
-    for i in range(3):
-        spread(slot_ref, rows_ref[i * 512 : (i + 1) * 512, :], tiles_ref, acc_ref, first + i)
+    spread(slot_ref, rows_ref, tiles_ref, acc_ref, core_ref[0])
     bsq_ref[...] = row_squares(rows_ref)
 
 
 def back_other_body(core_ref, slot_ref, rows_ref, acc_ref, bsq_ref, tiles_ref, msg_ref, acc):
-    first = 3 * (1 - core_ref[0])
     acc[...] = acc_ref[...]
-    for i in range(3):
-        spread(slot_ref, rows_ref[i * 512 : (i + 1) * 512, :], tiles_ref, acc, first + i)
+    spread(slot_ref, rows_ref, tiles_ref, acc, 1 - core_ref[0])
     tail = pack_row(row_squares(rows_ref) + bsq_ref[...], TAIL)
     write_pieces(msg_ref, tail, lambda p, lane: acc[p, :, lane : lane + LANES])
 
@@ -208,14 +203,14 @@
         fresh = fresh - across(beta / alpha) * prev_ref[...]
     if not last:
         refs[2][...] = fresh
-    narrow = fresh.astype(BF)
+    narrow = jnp.transpose(fresh).astype(BF)
     for q in range(32):
         msg_ref[q] = narrow
     bsq_ref[...] = bsq
 
 
 def square_body(g_ref, msg_ref):
-    tile = pack_row(squares(g_ref)).astype(BF)
+    tile = pack_row(column_squares(g_ref)).astype(BF)
     for i in range(8):
         msg_ref[i] = tile
 
@@ -248,58 +243,26 @@
     return jnp.concatenate(rows, axis=0), phi_bar
 
 
-def write_out(out_hbm, stage, sems, block):
+def final_body(*refs):
+    asq_ref = refs[7]
+    gathered = refs[8:12]
+    sol_hbm, search_hbm, phi_ref, stage, sems = refs[12:]
+    rows, phi_bar = coefficients(*refs[:7])
+    phi_ref[...] = phi_bar
+    alpha = jnp.sqrt(unpack_rows(asq_ref[...]) + EPS)
+    older = -alpha * rows[6:7] * rows[3:6]
+    newest = 1.0 / alpha
     copies = []
-    for i in range(8):
-        rows = pl.ds(i * 512, 512)
-        for q in range(4 * i, 4 * i + 4):
-            stage[q * 128 : (q + 1) * 128, :] = jnp.transpose(block(q))
-        copies.append(pltpu.make_async_copy(stage.at[rows], out_hbm.at[rows], sems.at[i]))
-        copies[-1].start()
+    for p in range(8):
+        at = pl.ds(p * 512, 512)
+        g0, g1, g2, g3 = [ref[p].astype(F32) for ref in gathered]
+        stage[0, at, :] = rows[0:1] * g0 + rows[1:2] * g1 + rows[2:3] * g2
+        stage[1, at, :] = older[0:1] * g0 + older[1:2] * g1 + older[2:3] * g2 + newest * g3
+        for i, out in enumerate((sol_hbm, search_hbm)):
+            copies.append(pltpu.make_async_copy(stage.at[i, at], out.at[at], sems.at[i, p]))
+            copies[-1].start()
     for c in copies:
         c.wait()
-
-
-def solution_body(*refs):
-    g0_ref, g1_ref, g2_ref, sol_hbm, coef_ref, phi_ref, stage, sems = refs[7:]
-    rows, phi_bar = coefficients(*refs[:7])
-    coef_ref[...] = rows
-    phi_ref[...] = phi_bar
-    wide = [across(rows[i : i + 1, :]) for i in range(3)]
-
-    def block(q):
-        out = wide[0] * g0_ref[q].astype(F32)
-        out = out + wide[1] * g1_ref[q].astype(F32)
-        return out + wide[2] * g2_ref[q].astype(F32)
-
-    write_out(sol_hbm, stage, sems, block)
-
-
-def search_body(coef_ref, asq_ref, g0_ref, g1_ref, g2_ref, g3_ref, search_hbm, stage, sems):
-    rows = coef_ref[...]
-    alpha = jnp.sqrt(unpack_rows(asq_ref[...]) + EPS)
-    shift = -alpha * rows[6:7, :]
-    wide = [across(shift * rows[3 + i : 4 + i, :]) for i in range(3)] + [across(1.0 / alpha)]
-
-    def block(q):
-        out = wide[0] * g0_ref[q].astype(F32)
-        out = out + wide[1] * g1_ref[q].astype(F32)
-        out = out + wide[2] * g2_ref[q].astype(F32)
-        return out + wide[3] * g3_ref[q].astype(F32)
-
-    write_out(search_hbm, stage, sems, block)
-
-
-def combine(body, count, smalls=()):
-    return pl.pallas_call(
-        body,
-        in_specs=[VM] * count,
-        out_specs=[ANY] + [VM] * len(smalls),
-        out_shape=[sds((4096, LANES), F32)] + list(smalls),
-        scratch_shapes=[pltpu.VMEM((4096, LANES), F32), pltpu.SemaphoreType.DMA((8,))],
-        compiler_params=pltpu.CompilerParams(vmem_limit_bytes=VMEM_LIMIT),
-        cost_estimate=pl.CostEstimate(flops=1 << 22, bytes_accessed=4 << 20, transcendentals=0),
-    )
 
 
 def per_device(readings, design_tiles, pattern):
@@ -333,7 +296,17 @@
     share = call(functools.partial(share_body, False, False), [VM] * 3, share_outs)
     share_last = call(functools.partial(share_body, False, True), [VM] * 3, share_outs[:2])
 
-    solve = combine(solution_body, 10, [sds((8, LANES), F32), row_type])
+    finish = pl.pallas_call(
+        final_body,
+        in_specs=[VM] * 12,
+        out_specs=[ANY, ANY, VM],
+        out_shape=[sds((4096, LANES), F32), sds((4096, LANES), F32), row_type],
+        scratch_shapes=[pltpu.VMEM((2, 4096, LANES), F32), pltpu.SemaphoreType.DMA((2, 8))],
+        compiler_params=pltpu.CompilerParams(vmem_limit_bytes=VMEM_LIMIT),
+    )
+
+    def gather(msg):
+        return over_sensor(msg).reshape(8, 512, LANES)
 
     def over_sensor(msg):
         return lax.all_to_all(msg, "sensor", 0, 0, tiled=True, axis_index_groups=S_GROUPS)
@@ -345,7 +318,7 @@
     slots, core, start = lax.optimization_barrier((slots, core, start))
     msg, tiles, left_rows = back_first(start, slots, readings, tiles)
     msg, bsq, r = share_first(over_sensor(msg))
-    gathered = [over_sensor(msg)]
+    gathered = [gather(msg)]
     bsqs = [bsq]
     asqs = []
     for sweep in range(ITERS):
@@ -368,13 +341,10 @@
         else:
             msg, bsq, r = share(over_sensor(msg), r, asq)
         bsqs.append(bsq)
-        if last:
-            sol, coef, phi_bar = solve(*bsqs, *asqs, *gathered)
-            msg, sol, phi_bar = lax.optimization_barrier((msg, sol, phi_bar))
-        gathered.append(over_sensor(msg))
+        gathered.append(gather(msg))
     (msg,) = call(square_body, [VM], [sds((8, EXTRA, LANES), BF)])(gathered[-1])
     msg = lax.all_to_all(msg, "basis", 0, 0, tiled=True)
-    (search,) = combine(search_body, 6)(coef, msg, *gathered)
+    sol, search, phi_bar = finish(*bsqs, *asqs, msg, *gathered)
     return sol, search, phi_bar.reshape(LANES)
 
 

time: 324 us -> 323 us (level)
  starting transfers between devices: 33 us -> 13.9 us
  blocking collectives: 259 us -> 277 us
    ppermute x3, starting transfers between devices: 23.6 us -> 5.42 us  [per_device(): other = lax.ppermute(own, 'basis', CORE_PERM)]
    all_to_all x6, blocking collectives: 80.2 us -> 97.8 us  [over_z(): lax.all_to_all(msg, 'basis', 0, 0, tiled=True, axis_index_groups=Z_GROUPS)]
where the time goes in v4:
time: 323 us; the launch traced here: 322 us
  blocking collectives  277 us (86%)
  Pallas kernels  25.6 us (8%)
  starting transfers between devices  13.9 us (4%)
  local copies, waits for them, and re-layouts  4.6 us (1%)
    all_to_all x8, blocking collectives, over_sensor(): lax.all_to_all(msg, 'sensor', 0, 0, tiled=True, axis_index_groups=S_GROUPS)  164 us
    all_to_all x6, blocking collectives, over_z(): lax.all_to_all(msg, 'basis', 0, 0, tiled=True, axis_index_groups=Z_GROUPS)  97.8 us
    all_to_all x1, blocking collectives, per_device(): msg = lax.all_to_all(msg, 'basis', 0, 0, tiled=True)  15.1 us
    ppermute x3, starting transfers between devices, per_device(): other = lax.ppermute(send, 'basis', CORE_PERM)  8.46 us
  transfers between devices with their start and end apart: 6, of which 0 were waited for; matrix products, arithmetic and copies ran while one was open for 0% of the time, Pallas kernels for 3%

profile of v4, /device:TPU:1, one launch (start us, length us, event | category | flops | bytes accessed | tf_op | source)
XLA Modules:
  0.0 322.4 jit_solution(2846936305674777991)
XLA Ops:
  0.6 0.0 copy-start
  0.6 2.8 copy-done
  3.4 0.0 copy-start.1
  3.4 1.1 copy-done.1
  4.6 0.0 copy-start.2
  4.6 0.7 copy-done.2
  5.2 2.3 shard_map.58
  7.5 25.4 %all_to_all.75.recv_ref = bf16[32,136,128]{2,1,0:T(8,128)(2,1)S(1)} all-to-all(bf16[32,136,128]{2,1,0:T(8,128)(2,1)S(1)} %get-tuple-element.45), channel_id=1, replica_groups={{192,128,64,0,208,144,80,16,224,160,96,32,240,176,112,48,200,136,72,8,2..., dimensions={0} | all-to-all | bytes 2228224 | tf_op jit(solution)/shard_map/all_to_all | solution.py:312
  33.0 0.3 shard_map.59
  33.3 0.0 copy-start.3
  33.3 19.3 %all_to_all.76 = bf16[32,128,128]{2,1,0:T(8,128)(2,1)S(1)} all-to-all(bf16[32,128,128]{2,1,0:T(8,128)(2,1)S(1)} %get-tuple-element.48), channel_id=1, replica_groups={{192,128,64,0,208,144,80,16,224,160,96,32,240,176,112,48,200,136,72,8,2..., dimensions={0} | all-to-all | bytes 2097152 | tf_op jit(solution)/shard_map/all_to_all | solution.py:312
  52.6 0.0 copy-done.3
  52.6 1.7 shard_map.61
  54.3 2.8 collective-permute-start
  57.1 1.5 shard_map.60.keep_ref
  58.7 0.0 collective-permute-done.recv_ref
  58.7 0.1 shard_map.62
  58.8 18.3 %all_to_all.77.recv_ref = bf16[4,400,128]{2,1,0:T(8,128)(2,1)S(1)} all-to-all(bf16[4,400,128]{2,1,0:T(8,128)(2,1)S(1)} %shard_map.62), channel_id=1, replica_groups={{6,4,2,0},{7,5,3,1},{14,12,10,8},{15,13,11,9},{22,20,18,16},{23,21,19,1..., dimensions={0} | all-to-all | bytes 819200 | tf_op jit(solution)/shard_map/all_to_all | solution.py:315
  77.1 0.1 shard_map.63
  77.2 16.1 %all_to_all.78 = bf16[4,384,128]{2,1,0:T(8,128)(2,1)S(1)} all-to-all(bf16[4,384,128]{2,1,0:T(8,128)(2,1)S(1)} %get-tuple-element.53), channel_id=1, replica_groups={{6,4,2,0},{7,5,3,1},{14,12,10,8},{15,13,11,9},{22,20,18,16},{23,21,19,1..., dimensions={0} | all-to-all | bytes 786432 | tf_op jit(solution)/shard_map/all_to_all | solution.py:315
  93.3 1.6 collective-permute-start.1
  94.9 1.4 shard_map.64
  96.3 0.0 collective-permute-done.1.rows_ref
  96.3 1.5 shard_map.65
  97.8 20.8 %all_to_all.79.recv_ref = bf16[32,136,128]{2,1,0:T(8,128)(2,1)S(1)} all-to-all(bf16[32,136,128]{2,1,0:T(8,128)(2,1)S(1)} %shard_map.65), channel_id=1, replica_groups={{192,128,64,0,208,144,80,16,224,160,96,32,240,176,112,48,200,136,72,8,2..., dimensions={0} | all-to-all | bytes 2228224 | tf_op jit(solution)/shard_map/all_to_all | solution.py:312
  118.6 0.3 shard_map.66
  119.0 19.0 %all_to_all.80 = bf16[32,128,128]{2,1,0:T(8,128)(2,1)S(1)} all-to-all(bf16[32,128,128]{2,1,0:T(8,128)(2,1)S(1)} %get-tuple-element.59), channel_id=1, replica_groups={{192,128,64,0,208,144,80,16,224,160,96,32,240,176,112,48,200,136,72,8,2..., dimensions={0} | all-to-all | bytes 2097152 | tf_op jit(solution)/shard_map/all_to_all | solution.py:312
  138.0 1.7 shard_map.68
  139.7 2.8 collective-permute-start.2
  142.5 1.5 shard_map.67.keep_ref
  144.1 0.0 collective-permute-done.2.recv_ref
  144.1 0.1 shard_map.69
  144.2 16.0 %all_to_all.81.recv_ref = bf16[4,400,128]{2,1,0:T(8,128)(2,1)S(1)} all-to-all(bf16[4,400,128]{2,1,0:T(8,128)(2,1)S(1)} %shard_map.69), channel_id=1, replica_groups={{6,4,2,0},{7,5,3,1},{14,12,10,8},{15,13,11,9},{22,20,18,16},{23,21,19,1..., dimensions={0} | all-to-all | bytes 819200 | tf_op jit(solution)/shard_map/all_to_all | solution.py:315
  160.2 0.1 shard_map.70
  160.3 15.7 %all_to_all.82 = bf16[4,384,128]{2,1,0:T(8,128)(2,1)S(1)} all-to-all(bf16[4,384,128]{2,1,0:T(8,128)(2,1)S(1)} %get-tuple-element.63), channel_id=1, replica_groups={{6,4,2,0},{7,5,3,1},{14,12,10,8},{15,13,11,9},{22,20,18,16},{23,21,19,1..., dimensions={0} | all-to-all | bytes 786432 | tf_op jit(solution)/shard_map/all_to_all | solution.py:315
  175.9 1.9 collective-permute-start.3
  177.9 1.4 shard_map.71
  179.2 0.0 collective-permute-done.3.rows_ref
  179.2 1.5 shard_map.72
  180.7 21.0 %all_to_all.83.recv_ref = bf16[32,136,128]{2,1,0:T(8,128)(2,1)S(1)} all-to-all(bf16[32,136,128]{2,1,0:T(8,128)(2,1)S(1)} %shard_map.72), channel_id=1, replica_groups={{192,128,64,0,208,144,80,16,224,160,96,32,240,176,112,48,200,136,72,8,2..., dimensions={0} | all-to-all | bytes 2228224 | tf_op jit(solution)/shard_map/all_to_all | solution.py:312
  201.7 0.3 shard_map.73
  202.1 19.0 %all_to_all.84 = bf16[32,128,128]{2,1,0:T(8,128)(2,1)S(1)} all-to-all(bf16[32,128,128]{2,1,0:T(8,128)(2,1)S(1)} %get-tuple-element.69), channel_id=1, replica_groups={{192,128,64,0,208,144,80,16,224,160,96,32,240,176,112,48,200,136,72,8,2..., dimensions={0} | all-to-all | bytes 2097152 | tf_op jit(solution)/shard_map/all_to_all | solution.py:312
  221.1 1.7 shard_map.75
  222.7 2.8 collective-permute-start.4
  225.6 1.5 shard_map.74.keep_ref
  227.1 0.0 collective-permute-done.4.recv_ref
  227.1 0.1 shard_map.76
  227.2 16.0 %all_to_all.85.recv_ref = bf16[4,400,128]{2,1,0:T(8,128)(2,1)S(1)} all-to-all(bf16[4,400,128]{2,1,0:T(8,128)(2,1)S(1)} %shard_map.76), channel_id=1, replica_groups={{6,4,2,0},{7,5,3,1},{14,12,10,8},{15,13,11,9},{22,20,18,16},{23,21,19,1..., dimensions={0} | all-to-all | bytes 819200 | tf_op jit(solution)/shard_map/all_to_all | solution.py:315
  243.3 0.1 shard_map.77
  243.3 15.6 %all_to_all.86 = bf16[4,384,128]{2,1,0:T(8,128)(2,1)S(1)} all-to-all(bf16[4,384,128]{2,1,0:T(8,128)(2,1)S(1)} %get-tuple-element.73), channel_id=1, replica_groups={{6,4,2,0},{7,5,3,1},{14,12,10,8},{15,13,11,9},{22,20,18,16},{23,21,19,1..., dimensions={0} | all-to-all | bytes 786432 | tf_op jit(solution)/shard_map/all_to_all | solution.py:315
  259.0 1.9 collective-permute-start.5
  260.9 1.4 shard_map.78
  262.2 0.0 collective-permute-done.5.rows_ref
  262.2 1.5 shard_map.79
  263.7 21.0 %all_to_all.87.recv_ref = bf16[32,136,128]{2,1,0:T(8,128)(2,1)S(1)} all-to-all(bf16[32,136,128]{2,1,0:T(8,128)(2,1)S(1)} %shard_map.79), channel_id=1, replica_groups={{192,128,64,0,208,144,80,16,224,160,96,32,240,176,112,48,200,136,72,8,2..., dimensions={0} | all-to-all | bytes 2228224 | tf_op jit(solution)/shard_map/all_to_all | solution.py:312
  284.7 0.3 shard_map.80
  285.1 19.0 %all_to_all.88 = bf16[32,128,128]{2,1,0:T(8,128)(2,1)S(1)} all-to-all(bf16[32,128,128]{2,1,0:T(8,128)(2,1)S(1)} %get-tuple-element.79), channel_id=1, replica_groups={{192,128,64,0,208,144,80,16,224,160,96,32,240,176,112,48,200,136,72,8,2..., dimensions={0} | all-to-all | bytes 2097152 | tf_op jit(solution)/shard_map/all_to_all | solution.py:312
  304.0 0.2 shard_map.81
  304.3 15.1 %all_to_all.89.refs_7_ = bf16[8,16,128]{2,1,0:T(8,128)(2,1)S(1)} all-to-all(bf16[8,16,128]{2,1,0:T(8,128)(2,1)S(1)} %shard_map.81), channel_id=1, replica_groups=mesh['sensor'=32,'basis'=8] {'basis'}, dimensions={0} | all-to-all | bytes 65536 | tf_op jit(solution)/shard_map/all_to_all | solution.py:346
  319.4 2.9 shard_map.82
Async XLA Ops:
  0.6 2.8 copy-start
  3.4 1.1 copy-start.1
  4.6 0.7 copy-start.2
  33.3 19.3 %copy-start.3 = (s32[3,1,2]{0,2,1:T(2,128)S(1)}, s32[3,1,2]{0,2,1:T(2,128)}, u32[]{:S(2)}) copy-start(s32[3,1,2]{0,2,1:T(2,128)} %param.5) | copy-start | bytes 76
  54.3 4.4 %collective-permute-start = (bf16[1552,128]{1,0:T(8,128)(2,1)S(1)}, bf16[1552,128]{1,0:T(8,128)(2,1)S(1)}, u32[]{:S(2)}, u32[]{:S(2)}) collective-permute-start(bf16[1552,128]{1,0:T(8,128)(2,1)S(1)} %get-tuple-element.50), channel_id=1, source_target_pairs={{0,1},{1,0},{2,3},{3,2},{4,5},{5,4},{6,7},{7,6},{8,9},{9,8},{10,11... | collective-permute-start | bytes 1191944 | tf_op jit(solution)/shard_map/ppermute | solution.py:327
  93.3 3.0 collective-permute-start.1
  139.7 4.4 %collective-permute-start.2 = (bf16[1552,128]{1,0:T(8,128)(2,1)S(1)}, bf16[1552,128]{1,0:T(8,128)(2,1)S(1)}, u32[]{:S(2)}, u32[]{:S(2)}) collective-permute-start(bf16[1552,128]{1,0:T(8,128)(2,1)S(1)} %get-tuple-element.60), channel_id=1, source_target_pairs={{0,1},{1,0},{2,3},{3,2},{4,5},{5,4},{6,7},{7,6},{8,9},{9,8},{10,11... | collective-permute-start | bytes 1191944 | tf_op jit(solution)/shard_map/ppermute | solution.py:327
  175.9 3.3 %collective-permute-start.3 = (bf16[1536,128]{1,0:T(8,128)(2,1)S(1)}, bf16[1536,128]{1,0:T(8,128)(2,1)S(1)}, u32[]{:S(2)}, u32[]{:S(2)}) collective-permute-start(bf16[1536,128]{1,0:T(8,128)(2,1)S(1)} %bitcast.28), channel_id=1, source_target_pairs={{0,1},{1,0},{2,3},{3,2},{4,5},{5,4},{6,7},{7,6},{8,9},{9,8},{10,11... | collective-permute-start | bytes 1179656 | tf_op jit(solution)/shard_map/ppermute | solution.py:336
  222.7 4.4 %collective-permute-start.4 = (bf16[1552,128]{1,0:T(8,128)(2,1)S(1)}, bf16[1552,128]{1,0:T(8,128)(2,1)S(1)}, u32[]{:S(2)}, u32[]{:S(2)}) collective-permute-start(bf16[1552,128]{1,0:T(8,128)(2,1)S(1)} %get-tuple-element.70), channel_id=1, source_target_pairs={{0,1},{1,0},{2,3},{3,2},{4,5},{5,4},{6,7},{7,6},{8,9},{9,8},{10,11... | collective-permute-start | bytes 1191944 | tf_op jit(solution)/shard_map/ppermute | solution.py:327
  259.0 3.3 %collective-permute-start.5 = (bf16[1536,128]{1,0:T(8,128)(2,1)S(1)}, bf16[1536,128]{1,0:T(8,128)(2,1)S(1)}, u32[]{:S(2)}, u32[]{:S(2)}) collective-permute-start(bf16[1536,128]{1,0:T(8,128)(2,1)S(1)} %bitcast.30), channel_id=1, source_target_pairs={{0,1},{1,0},{2,3},{3,2},{4,5},{5,4},{6,7},{7,6},{8,9},{9,8},{10,11... | collective-permute-start | bytes 1179656 | tf_op jit(solution)/shard_map/ppermute | solution.py:336

commit v5 on v4

--- a/solution.py
+++ b/solution.py
@@ -18,7 +18,7 @@
 BF = jnp.bfloat16
 F32 = jnp.float32
 Z_GROUPS = [[6, 4, 2, 0], [7, 5, 3, 1]]
-S_GROUPS = [[(y * 4 + x) * 2 + z for z in range(2) for x in range(4) for y in (3, 2, 1, 0)]]
+S_GROUPS = [[(y * 4 + x) * 2 + z for z in range(2) for x in (3, 2, 1, 0) for y in (3, 2, 1, 0)]]
 CORE_PERM = [(i, i ^ 1) for i in range(8)]
 
 VM = pl.BlockSpec(memory_space=pltpu.VMEM)
@@ -30,13 +30,14 @@
     return jax.ShapeDtypeStruct(shape, dtype)
 
 
-def call(body, ins, outs, scratch=(), flops=0):
+def call(body, ins, outs, scratch=(), flops=0, aliases=None):
     return pl.pallas_call(
         body,
         in_specs=ins,
         out_specs=[VM] * len(outs),
         out_shape=outs,
         scratch_shapes=scratch,
+        input_output_aliases=aliases or {},
         compiler_params=pltpu.CompilerParams(vmem_limit_bytes=VMEM_LIMIT),
         cost_estimate=pl.CostEstimate(
             flops=int(flops), bytes_accessed=(4 << 20) if flops else (1 << 20), transcendentals=0
@@ -181,7 +182,6 @@
 
 
 def back_other_body(core_ref, slot_ref, rows_ref, acc_ref, bsq_ref, tiles_ref, msg_ref, acc):
-    acc[...] = acc_ref[...]
     spread(slot_ref, rows_ref, tiles_ref, acc, 1 - core_ref[0])
     tail = pack_row(row_squares(rows_ref) + bsq_ref[...], TAIL)
     write_pieces(msg_ref, tail, lambda p, lane: acc[p, :, lane : lane + LANES])
@@ -290,7 +290,9 @@
         flops=8e8,
     )
     back_own = call(back_own_body, [SM, SM, VM, VM], [acc_type, row_type], flops=4e8)
-    back_other = call(back_other_body, [SM, SM, VM, VM, VM, VM], [msg_type], [acc_buf], flops=4e8)
+    back_other = call(
+        back_other_body, [SM, SM, VM, VM, VM, VM], [msg_type, acc_type], flops=4e8, aliases={3: 1}
+    )
     share_outs = [sds((32, LANES, LANES), BF), row_type, sds((LANES, LANES), F32)]
     share_first = call(functools.partial(share_body, True, False), [VM], share_outs)
     share = call(functools.partial(share_body, False, False), [VM] * 3, share_outs)
@@ -335,7 +337,7 @@
         own = over_z(msg).reshape(1536, LANES)
         other = lax.ppermute(own, "basis", CORE_PERM)
         acc, own_bsq = back_own(core, slots, own, tiles)
-        (msg,) = back_other(core, slots, other, acc, own_bsq, tiles)
+        msg, _ = back_other(core, slots, other, acc, own_bsq, tiles)
         if last:
             msg, bsq = share_last(over_sensor(msg), r, asq)
         else:

time: 323 us -> 322 us (level)
  blocking collectives: 277 us -> 265 us
  starting transfers between devices: 13.9 us -> 25.6 us
    all_to_all x6, blocking collectives: 97.8 us -> 82.2 us  [over_z(): lax.all_to_all(msg, 'basis', 0, 0, tiled=True, axis_index_groups=Z_GROUPS)]
    ppermute x3, starting transfers between devices: 5.42 us -> 15.6 us  [per_device(): other = lax.ppermute(own, 'basis', CORE_PERM)]
where the time goes in v5:
time: 322 us
  blocking collectives  265 us (82%)
  starting transfers between devices  25.6 us (8%)
  Pallas kernels  25 us (8%)
  local copies, waits for them, and re-layouts  4.59 us (1%)
    all_to_all x8, blocking collectives, over_sensor(): lax.all_to_all(msg, 'sensor', 0, 0, tiled=True, axis_index_groups=S_GROUPS)  168 us
    all_to_all x6, blocking collectives, over_z(): lax.all_to_all(msg, 'basis', 0, 0, tiled=True, axis_index_groups=Z_GROUPS)  82.2 us
    ppermute x3, starting transfers between devices, per_device(): other = lax.ppermute(own, 'basis', CORE_PERM)  15.6 us
    all_to_all x1, blocking collectives, per_device(): msg = lax.all_to_all(msg, 'basis', 0, 0, tiled=True)  15.6 us
    ppermute x3, starting transfers between devices, per_device(): other = lax.ppermute(send, 'basis', CORE_PERM)  9.98 us
  transfers between devices with their start and end apart: 6, of which 0 were waited for; matrix products, arithmetic and copies ran while one was open for 0% of the time, Pallas kernels for 3%

profile of v5, /device:TPU:1, one launch (start us, length us, event | category | flops | bytes accessed | tf_op | source)
XLA Modules:
  0.0 321.6 jit_solution(4535335665143720413)
XLA Ops:
  0.6 0.0 copy-start
  0.6 2.8 copy-done
  3.4 0.0 copy-start.1
  3.4 1.1 copy-done.1
  4.6 0.0 copy-start.2
  4.6 0.7 copy-done.2
  5.2 2.3 shard_map.58
  7.5 24.6 %all_to_all.75.recv_ref = bf16[32,136,128]{2,1,0:T(8,128)(2,1)S(1)} all-to-all(bf16[32,136,128]{2,1,0:T(8,128)(2,1)S(1)} %get-tuple-element.48), channel_id=1, replica_groups={{240,176,112,48,224,160,96,32,208,144,80,16,192,128,64,0,248,184,120,56..., dimensions={0} | all-to-all | bytes 2228224 | tf_op jit(solution)/shard_map/all_to_all | solution.py:314
  32.1 0.0 copy-start.3
  32.1 0.3 shard_map.59
  32.5 19.1 %all_to_all.76 = bf16[32,128,128]{2,1,0:T(8,128)(2,1)S(1)} all-to-all(bf16[32,128,128]{2,1,0:T(8,128)(2,1)S(1)} %get-tuple-element.51), channel_id=1, replica_groups={{240,176,112,48,224,160,96,32,208,144,80,16,192,128,64,0,248,184,120,56..., dimensions={0} | all-to-all | bytes 2097152 | tf_op jit(solution)/shard_map/all_to_all | solution.py:314
  51.6 0.0 copy-done.3
  51.6 1.7 shard_map.61
  53.3 3.4 %collective-permute-start = (bf16[1552,128]{1,0:T(8,128)(2,1)S(1)}, bf16[1552,128]{1,0:T(8,128)(2,1)S(1)}, u32[]{:S(2)}, u32[]{:S(2)}) collective-permute-start(bf16[1552,128]{1,0:T(8,128)(2,1)S(1)} %get-tuple-element.53), channel_id=1, source_target_pairs={{0,1},{1,0},{2,3},{3,2},{4,5},{5,4},{6,7},{7,6},{8,9},{9,8},{10,11... | collective-permute-start | bytes 1191944 | tf_op jit(solution)/shard_map/ppermute | solution.py:329
  56.6 1.5 shard_map.60.keep_ref
  58.2 0.0 collective-permute-done.recv_ref
  58.2 0.1 shard_map.62
  58.3 16.5 %all_to_all.77.recv_ref = bf16[4,400,128]{2,1,0:T(8,128)(2,1)S(1)} all-to-all(bf16[4,400,128]{2,1,0:T(8,128)(2,1)S(1)} %shard_map.62), channel_id=1, replica_groups={{6,4,2,0},{7,5,3,1},{14,12,10,8},{15,13,11,9},{22,20,18,16},{23,21,19,1..., dimensions={0} | all-to-all | bytes 819200 | tf_op jit(solution)/shard_map/all_to_all | solution.py:317
  74.8 0.1 shard_map.63
  74.9 12.5 %all_to_all.78 = bf16[4,384,128]{2,1,0:T(8,128)(2,1)S(1)} all-to-all(bf16[4,384,128]{2,1,0:T(8,128)(2,1)S(1)} %get-tuple-element.56), channel_id=1, replica_groups={{6,4,2,0},{7,5,3,1},{14,12,10,8},{15,13,11,9},{22,20,18,16},{23,21,19,1..., dimensions={0} | all-to-all | bytes 786432 | tf_op jit(solution)/shard_map/all_to_all | solution.py:317
  87.4 6.5 %collective-permute-start.1 = (bf16[1536,128]{1,0:T(8,128)(2,1)S(1)}, bf16[1536,128]{1,0:T(8,128)(2,1)S(1)}, u32[]{:S(2)}, u32[]{:S(2)}) collective-permute-start(bf16[1536,128]{1,0:T(8,128)(2,1)S(1)} %bitcast.26), channel_id=1, source_target_pairs={{0,1},{1,0},{2,3},{3,2},{4,5},{5,4},{6,7},{7,6},{8,9},{9,8},{10,11... | collective-permute-start | bytes 1179656 | tf_op jit(solution)/shard_map/ppermute | solution.py:338
  93.9 1.4 shard_map.64
  95.3 0.0 collective-permute-done.1.rows_ref
  95.3 1.3 shard_map.65
  96.6 21.3 %all_to_all.79.recv_ref = bf16[32,136,128]{2,1,0:T(8,128)(2,1)S(1)} all-to-all(bf16[32,136,128]{2,1,0:T(8,128)(2,1)S(1)} %get-tuple-element.59), channel_id=1, replica_groups={{240,176,112,48,224,160,96,32,208,144,80,16,192,128,64,0,248,184,120,56..., dimensions={0} | all-to-all | bytes 2228224 | tf_op jit(solution)/shard_map/all_to_all | solution.py:314
  117.9 0.3 shard_map.66
  118.3 18.6 %all_to_all.80 = bf16[32,128,128]{2,1,0:T(8,128)(2,1)S(1)} all-to-all(bf16[32,128,128]{2,1,0:T(8,128)(2,1)S(1)} %get-tuple-element.63), channel_id=1, replica_groups={{240,176,112,48,224,160,96,32,208,144,80,16,192,128,64,0,248,184,120,56..., dimensions={0} | all-to-all | bytes 2097152 | tf_op jit(solution)/shard_map/all_to_all | solution.py:314
  136.8 1.7 shard_map.68
  138.5 3.3 %collective-permute-start.2 = (bf16[1552,128]{1,0:T(8,128)(2,1)S(1)}, bf16[1552,128]{1,0:T(8,128)(2,1)S(1)}, u32[]{:S(2)}, u32[]{:S(2)}) collective-permute-start(bf16[1552,128]{1,0:T(8,128)(2,1)S(1)} %get-tuple-element.64), channel_id=1, source_target_pairs={{0,1},{1,0},{2,3},{3,2},{4,5},{5,4},{6,7},{7,6},{8,9},{9,8},{10,11... | collective-permute-start | bytes 1191944 | tf_op jit(solution)/shard_map/ppermute | solution.py:329
  141.8 1.5 shard_map.67.keep_ref
  143.4 0.0 collective-permute-done.2.recv_ref
  143.4 0.1 shard_map.69
  143.5 14.3 %all_to_all.81.recv_ref = bf16[4,400,128]{2,1,0:T(8,128)(2,1)S(1)} all-to-all(bf16[4,400,128]{2,1,0:T(8,128)(2,1)S(1)} %shard_map.69), channel_id=1, replica_groups={{6,4,2,0},{7,5,3,1},{14,12,10,8},{15,13,11,9},{22,20,18,16},{23,21,19,1..., dimensions={0} | all-to-all | bytes 819200 | tf_op jit(solution)/shard_map/all_to_all | solution.py:317
  157.8 0.1 shard_map.70
  157.9 12.3 %all_to_all.82 = bf16[4,384,128]{2,1,0:T(8,128)(2,1)S(1)} all-to-all(bf16[4,384,128]{2,1,0:T(8,128)(2,1)S(1)} %get-tuple-element.67), channel_id=1, replica_groups={{6,4,2,0},{7,5,3,1},{14,12,10,8},{15,13,11,9},{22,20,18,16},{23,21,19,1..., dimensions={0} | all-to-all | bytes 786432 | tf_op jit(solution)/shard_map/all_to_all | solution.py:317
  170.3 4.5 %collective-permute-start.3 = (bf16[1536,128]{1,0:T(8,128)(2,1)S(1)}, bf16[1536,128]{1,0:T(8,128)(2,1)S(1)}, u32[]{:S(2)}, u32[]{:S(2)}) collective-permute-start(bf16[1536,128]{1,0:T(8,128)(2,1)S(1)} %bitcast.28), channel_id=1, source_target_pairs={{0,1},{1,0},{2,3},{3,2},{4,5},{5,4},{6,7},{7,6},{8,9},{9,8},{10,11... | collective-permute-start | bytes 1179656 | tf_op jit(solution)/shard_map/ppermute | solution.py:338
  174.8 1.4 shard_map.71
  176.2 0.0 collective-permute-done.3.rows_ref
  176.2 1.3 shard_map.72
  177.5 23.4 %all_to_all.83.recv_ref = bf16[32,136,128]{2,1,0:T(8,128)(2,1)S(1)} all-to-all(bf16[32,136,128]{2,1,0:T(8,128)(2,1)S(1)} %get-tuple-element.70), channel_id=1, replica_groups={{240,176,112,48,224,160,96,32,208,144,80,16,192,128,64,0,248,184,120,56..., dimensions={0} | all-to-all | bytes 2228224 | tf_op jit(solution)/shard_map/all_to_all | solution.py:314
  200.9 0.3 shard_map.73
  201.3 18.6 %all_to_all.84 = bf16[32,128,128]{2,1,0:T(8,128)(2,1)S(1)} all-to-all(bf16[32,128,128]{2,1,0:T(8,128)(2,1)S(1)} %get-tuple-element.74), channel_id=1, replica_groups={{240,176,112,48,224,160,96,32,208,144,80,16,192,128,64,0,248,184,120,56..., dimensions={0} | all-to-all | bytes 2097152 | tf_op jit(solution)/shard_map/all_to_all | solution.py:314
  219.8 1.7 shard_map.75
  221.5 3.3 %collective-permute-start.4 = (bf16[1552,128]{1,0:T(8,128)(2,1)S(1)}, bf16[1552,128]{1,0:T(8,128)(2,1)S(1)}, u32[]{:S(2)}, u32[]{:S(2)}) collective-permute-start(bf16[1552,128]{1,0:T(8,128)(2,1)S(1)} %get-tuple-element.75), channel_id=1, source_target_pairs={{0,1},{1,0},{2,3},{3,2},{4,5},{5,4},{6,7},{7,6},{8,9},{9,8},{10,11... | collective-permute-start | bytes 1191944 | tf_op jit(solution)/shard_map/ppermute | solution.py:329
  224.8 1.5 shard_map.74.keep_ref
  226.4 0.0 collective-permute-done.4.recv_ref
  226.4 0.1 shard_map.76
  226.5 14.2 %all_to_all.85.recv_ref = bf16[4,400,128]{2,1,0:T(8,128)(2,1)S(1)} all-to-all(bf16[4,400,128]{2,1,0:T(8,128)(2,1)S(1)} %shard_map.76), channel_id=1, replica_groups={{6,4,2,0},{7,5,3,1},{14,12,10,8},{15,13,11,9},{22,20,18,16},{23,21,19,1..., dimensions={0} | all-to-all | bytes 819200 | tf_op jit(solution)/shard_map/all_to_all | solution.py:317
  240.8 0.1 shard_map.77
  240.8 12.3 %all_to_all.86 = bf16[4,384,128]{2,1,0:T(8,128)(2,1)S(1)} all-to-all(bf16[4,384,128]{2,1,0:T(8,128)(2,1)S(1)} %get-tuple-element.78), channel_id=1, replica_groups={{6,4,2,0},{7,5,3,1},{14,12,10,8},{15,13,11,9},{22,20,18,16},{23,21,19,1..., dimensions={0} | all-to-all | bytes 786432 | tf_op jit(solution)/shard_map/all_to_all | solution.py:317
  253.1 4.6 %collective-permute-start.5 = (bf16[1536,128]{1,0:T(8,128)(2,1)S(1)}, bf16[1536,128]{1,0:T(8,128)(2,1)S(1)}, u32[]{:S(2)}, u32[]{:S(2)}) collective-permute-start(bf16[1536,128]{1,0:T(8,128)(2,1)S(1)} %bitcast.30), channel_id=1, source_target_pairs={{0,1},{1,0},{2,3},{3,2},{4,5},{5,4},{6,7},{7,6},{8,9},{9,8},{10,11... | collective-permute-start | bytes 1179656 | tf_op jit(solution)/shard_map/ppermute | solution.py:338
  257.7 1.4 shard_map.78
  259.1 0.0 collective-permute-done.5.rows_ref
  259.1 1.3 shard_map.79
  260.4 23.4 %all_to_all.87.recv_ref = bf16[32,136,128]{2,1,0:T(8,128)(2,1)S(1)} all-to-all(bf16[32,136,128]{2,1,0:T(8,128)(2,1)S(1)} %get-tuple-element.81), channel_id=1, replica_groups={{240,176,112,48,224,160,96,32,208,144,80,16,192,128,64,0,248,184,120,56..., dimensions={0} | all-to-all | bytes 2228224 | tf_op jit(solution)/shard_map/all_to_all | solution.py:314
  283.8 0.3 shard_map.80
  284.1 18.6 %all_to_all.88 = bf16[32,128,128]{2,1,0:T(8,128)(2,1)S(1)} all-to-all(bf16[32,128,128]{2,1,0:T(8,128)(2,1)S(1)} %get-tuple-element.85), channel_id=1, replica_groups={{240,176,112,48,224,160,96,32,208,144,80,16,192,128,64,0,248,184,120,56..., dimensions={0} | all-to-all | bytes 2097152 | tf_op jit(solution)/shard_map/all_to_all | solution.py:314
  302.7 0.2 shard_map.81
  303.0 15.6 %all_to_all.89.refs_7_ = bf16[8,16,128]{2,1,0:T(8,128)(2,1)S(1)} all-to-all(bf16[8,16,128]{2,1,0:T(8,128)(2,1)S(1)} %shard_map.81), channel_id=1, replica_groups=mesh['sensor'=32,'basis'=8] {'basis'}, dimensions={0} | all-to-all | bytes 65536 | tf_op jit(solution)/shard_map/all_to_all | solution.py:348
  318.5 2.9 shard_map.82
Async XLA Ops:
  0.6 2.8 copy-start
  3.4 1.1 copy-start.1
  4.6 0.7 copy-start.2
  32.1 19.5 %copy-start.3 = (s32[3,1,2]{0,2,1:T(2,128)S(1)}, s32[3,1,2]{0,2,1:T(2,128)}, u32[]{:S(2)}) copy-start(s32[3,1,2]{0,2,1:T(2,128)} %param.5) | copy-start | bytes 76
  53.3 4.9 %collective-permute-start = (bf16[1552,128]{1,0:T(8,128)(2,1)S(1)}, bf16[1552,128]{1,0:T(8,128)(2,1)S(1)}, u32[]{:S(2)}, u32[]{:S(2)}) collective-permute-start(bf16[1552,128]{1,0:T(8,128)(2,1)S(1)} %get-tuple-element.53), channel_id=1, source_target_pairs={{0,1},{1,0},{2,3},{3,2},{4,5},{5,4},{6,7},{7,6},{8,9},{9,8},{10,11... | collective-permute-start | bytes 1191944 | tf_op jit(solution)/shard_map/ppermute | solution.py:329
  87.4 7.9 %collective-permute-start.1 = (bf16[1536,128]{1,0:T(8,128)(2,1)S(1)}, bf16[1536,128]{1,0:T(8,128)(2,1)S(1)}, u32[]{:S(2)}, u32[]{:S(2)}) collective-permute-start(bf16[1536,128]{1,0:T(8,128)(2,1)S(1)} %bitcast.26), channel_id=1, source_target_pairs={{0,1},{1,0},{2,3},{3,2},{4,5},{5,4},{6,7},{7,6},{8,9},{9,8},{10,11... | collective-permute-start | bytes 1179656 | tf_op jit(solution)/shard_map/ppermute | solution.py:338
  138.5 4.9 %collective-permute-start.2 = (bf16[1552,128]{1,0:T(8,128)(2,1)S(1)}, bf16[1552,128]{1,0:T(8,128)(2,1)S(1)}, u32[]{:S(2)}, u32[]{:S(2)}) collective-permute-start(bf16[1552,128]{1,0:T(8,128)(2,1)S(1)} %get-tuple-element.64), channel_id=1, source_target_pairs={{0,1},{1,0},{2,3},{3,2},{4,5},{5,4},{6,7},{7,6},{8,9},{9,8},{10,11... | collective-permute-start | bytes 1191944 | tf_op jit(solution)/shard_map/ppermute | solution.py:329
  170.3 5.9 %collective-permute-start.3 = (bf16[1536,128]{1,0:T(8,128)(2,1)S(1)}, bf16[1536,128]{1,0:T(8,128)(2,1)S(1)}, u32[]{:S(2)}, u32[]{:S(2)}) collective-permute-start(bf16[1536,128]{1,0:T(8,128)(2,1)S(1)} %bitcast.28), channel_id=1, source_target_pairs={{0,1},{1,0},{2,3},{3,2},{4,5},{5,4},{6,7},{7,6},{8,9},{9,8},{10,11... | collective-permute-start | bytes 1179656 | tf_op jit(solution)/shard_map/ppermute | solution.py:338
  221.5 4.9 %collective-permute-start.4 = (bf16[1552,128]{1,0:T(8,128)(2,1)S(1)}, bf16[1552,128]{1,0:T(8,128)(2,1)S(1)}, u32[]{:S(2)}, u32[]{:S(2)}) collective-permute-start(bf16[1552,128]{1,0:T(8,128)(2,1)S(1)} %get-tuple-element.75), channel_id=1, source_target_pairs={{0,1},{1,0},{2,3},{3,2},{4,5},{5,4},{6,7},{7,6},{8,9},{9,8},{10,11... | collective-permute-start | bytes 1191944 | tf_op jit(solution)/shard_map/ppermute | solution.py:329
  253.1 5.9 %collective-permute-start.5 = (bf16[1536,128]{1,0:T(8,128)(2,1)S(1)}, bf16[1536,128]{1,0:T(8,128)(2,1)S(1)}, u32[]{:S(2)}, u32[]{:S(2)}) collective-permute-start(bf16[1536,128]{1,0:T(8,128)(2,1)S(1)} %bitcast.30), channel_id=1, source_target_pairs={{0,1},{1,0},{2,3},{3,2},{4,5},{5,4},{6,7},{7,6},{8,9},{9,8},{10,11... | collective-permute-start | bytes 1179656 | tf_op jit(solution)/shard_map/ppermute | solution.py:338
